TPU v7x, 256 devices: a whole 4x4x8 slice. The times are simulated.
256 devices in a mesh: branch: 2 (over core), seq: 16 (over z, y_hi), fsdp: 8 (over y_lo, x).
Axes of the slice: x: 4, y: 4 (y_hi: 2, y_lo: 2; y = y_hi * 2 + y_lo), z: 8, core: 2. Of those that a mesh axis runs over, the one named last changes fastest.
Arguments:
- latents: bfloat16 [3072, 5120], P('seq'), may hold values from -6 to 6
- noise: bfloat16 [2, 3072, 5120], P(None, 'seq'), may hold values from -6 to 6
- time_index: int32 [2], replicated, may hold values from 20 to 979
- cfg_pair: int32 [2], replicated, may hold values from 0 to 15
- cond_table: float32 [16, 5120], replicated, may hold values from -6 to 6
- gain: float32 [2, 5120], P('branch'), may hold values from 0.5 to 1.5
- w_qkv: bfloat16 [2, 3, 5120, 3072], P('branch', None, 'seq', 'fsdp'), may hold values from -0.5 to 0.5
- w_out: bfloat16 [2, 3072, 5120], P('branch', 'fsdp', 'seq'), may hold values from -0.109375 to 0.109375
Outputs:
- dmd_grad: float32 [3072, 5120], P('seq', ('branch', 'fsdp'))
- critic_residual: float32 [3072, 5120], P('seq', ('branch', 'fsdp'))
All inputs are finite; a program needn't handle non-finite values.
Results may differ from a plain program's by a relative error of at most 0.013.
Values may be sent and summed in bfloat16 or wider, within the bound.
A program may use at most 128 MiB of HBM per device.

v0:
```python
import jax
import jax.numpy as jnp
from jax import lax
from jax.sharding import Mesh
from jax.sharding import PartitionSpec as P

HD = 128
SEQ = ("seq_0", "seq_1")


GUIDANCE = 3.5
EPSILON = 1e-06


def whole_of(x, axes, dim):
    if not axes:
        return x
    nearer = lax.all_gather(x, axes[-1], axis=dim, tiled=True)
    return whole_of(nearer, axes[:-1], dim)


def sent_together(arrays, axis, dim, along):
    ends, at = ([], 0)
    for a in arrays[:-1]:
        at += a.shape[along]
        ends.append(at)
    both = jnp.concatenate(arrays, axis=along)
    return tuple(jnp.split(lax.all_gather(both, axis, axis=dim, tiled=True), ends, axis=along))


def in_blocks(x, dim, count):
    before, after = (x.shape[:dim], x.shape[dim + 1 :])
    return jnp.moveaxis(x.reshape(*before, count, -1, *after), dim, 0)


def sent_and_summed(x, axis, dim):
    count = lax.axis_size(axis)
    blocks = lax.all_to_all(in_blocks(x, dim, count), axis, 0, 0, tiled=True)
    return jnp.sum(blocks.astype(jnp.float32), axis=0)


def partner(x, axis, distance):
    return lax.ppermute(x, axis, [(i, i ^ 1 << distance) for i in range(lax.axis_size(axis))])


def sigma_of(step_index):
    fraction = step_index.astype(jnp.float32) / 1000.0
    return 5.0 * fraction / (1.0 + 4.0 * fraction)


def noisy_mix(tokens, noise_rows, step_index):
    noise_level = sigma_of(step_index)
    return (1.0 - noise_level) * tokens + noise_level * noise_rows.astype(jnp.float32)


def normed(noisy_rows, gain_row, shift_row):
    mean_square = jnp.mean(noisy_rows * noisy_rows, axis=-1, keepdims=True)
    return (noisy_rows * lax.rsqrt(mean_square + EPSILON) * gain_row + shift_row).astype(
        jnp.bfloat16
    )


def table_row(cond_table, cond_row):
    one_hot = (jnp.arange(cond_table.shape[0], dtype=jnp.int32) == cond_row).astype(jnp.float32)
    return jnp.dot(one_hot, cond_table, precision=lax.Precision.HIGHEST)


def attend_init(queries):
    passes, tok_rows, local_heads = (queries.shape[0], queries.shape[1], queries.shape[2])
    peak_score = jnp.full((passes, tok_rows, local_heads), -1e30, jnp.float32)
    mass_total = jnp.zeros((passes, tok_rows, local_heads), jnp.float32)
    accum = jnp.zeros(queries.shape, jnp.float32)
    return (peak_score, mass_total, accum)


def make_absorb(queries, carry, block_rows):
    local_heads = queries.shape[2]
    peak_score, mass_total, accum = carry
    key_rows, value_rows = block_rows
    passes, key_count = (key_rows.shape[0], key_rows.shape[1])
    key_rows = key_rows.reshape(passes, key_count, local_heads, HD)
    value_rows = value_rows.reshape(passes, key_count, local_heads, HD)
    scores = jnp.einsum(
        "pqhd,prhd->pqhr", queries, key_rows, preferred_element_type=jnp.float32
    ) * HD ** (-0.5)
    new_peak = jnp.maximum(peak_score, jnp.max(scores, axis=-1))
    softmax_w = jnp.exp(scores - new_peak[..., None])
    mass_total = jnp.sum(softmax_w, axis=-1)
    accum = jnp.einsum(
        "pqhr,prhd->pqhd",
        softmax_w.astype(jnp.bfloat16),
        value_rows,
        preferred_element_type=jnp.float32,
    )
    return (new_peak, mass_total, accum)


def finish(carry):
    peak_score, mass_total, accum = carry
    return (accum / mass_total[..., None]).astype(jnp.bfloat16)


def body(latents, noise, time_index, cfg_pair, cond_table, gain, w_qkv, w_out):
    branch = lax.axis_index("branch")
    fsdp_count = lax.axis_size("fsdp")
    tok_rows = latents.shape[0]
    tokens = latents.astype(jnp.float32)
    noisy_main = noisy_mix(tokens, noise[0], time_index[0])
    own_noise = lax.dynamic_index_in_dim(noise, branch, 0, keepdims=False)
    own_index = lax.dynamic_index_in_dim(time_index, branch, 0, keepdims=False)
    noisy_own = noisy_mix(tokens, own_noise, own_index)
    cond_shift = table_row(cond_table, cfg_pair[0])
    second_row = lax.dynamic_index_in_dim(cfg_pair, 1 - branch, 0, keepdims=False)
    second_shift = table_row(cond_table, second_row)
    gain_row = gain[0]
    inputs = jnp.stack(
        [normed(noisy_main, gain_row, cond_shift), normed(noisy_own, gain_row, second_shift)]
    )
    weights = w_qkv[0]
    col_count = weights.shape[2]
    local_heads = col_count // HD
    projected = jnp.einsum(
        "ptd,jdc->pjtc",
        inputs,
        lax.all_gather(weights, SEQ, axis=1, tiled=True),
        preferred_element_type=jnp.float32,
    ).astype(jnp.bfloat16)
    out_full = whole_of(w_out[0], SEQ, 1)
    queries = projected[:, 0].reshape(2, tok_rows, local_heads, HD)
    key_all = projected[:, 1]
    value_all = projected[:, 2]
    state = make_absorb(
        queries, attend_init(queries), sent_together((key_all, value_all), SEQ, 1, 0)
    )
    attn = finish(state)
    attn = attn.reshape(2, tok_rows, col_count)
    partial_value = jnp.einsum("ptc,cd->ptd", attn, out_full, preferred_element_type=jnp.float32)
    width_all = partial_value.shape[2]
    half_width = width_all // (2 * fsdp_count)
    partial_value = (
        partial_value.reshape(2, tok_rows, 2, fsdp_count, half_width)
        .transpose(0, 1, 3, 2, 4)
        .reshape(2, tok_rows, width_all)
    )
    head_sums = sent_and_summed(partial_value.astype(jnp.bfloat16), "fsdp", 2)
    own_half = lax.dynamic_slice_in_dim(head_sums, branch * half_width, half_width, 2)
    give_half = lax.dynamic_slice_in_dim(head_sums, (1 - branch) * half_width, half_width, 2)
    partner_first, partner_second = (
        partner(give_half[0].astype(jnp.bfloat16), "branch", 0).astype(jnp.float32),
        partner(give_half[1].astype(jnp.bfloat16), "branch", 0).astype(jnp.float32),
    )
    own_first, own_second = (own_half[0], own_half[1])
    is_teacher = branch == 0
    teacher_cond = jnp.where(is_teacher, own_first, partner_first)
    teacher_null = jnp.where(is_teacher, own_second, partner_second)
    critic_main = jnp.where(is_teacher, partner_first, own_first)
    critic_own = jnp.where(is_teacher, partner_second, own_second)
    dmd_grad = critic_main - (teacher_null + GUIDANCE * (teacher_cond - teacher_null))
    col_start = (branch * fsdp_count + lax.axis_index("fsdp")) * half_width
    noise_cols = lax.dynamic_slice_in_dim(noise[1], col_start, half_width, 1).astype(jnp.float32)
    latent_cols = lax.dynamic_slice_in_dim(latents, col_start, half_width, 1).astype(jnp.float32)
    critic_residual = critic_own - (noise_cols - latent_cols)
    return (dmd_grad, critic_residual)


def solution(mesh):
    torus = Mesh(
        mesh.devices.reshape(mesh.shape["branch"], 8, 2, mesh.shape["fsdp"]),
        ("branch", "seq_0", "seq_1", "fsdp"),
    )
    return jax.shard_map(
        body,
        mesh=torus,
        in_specs=(
            P(SEQ, None),
            P(None, SEQ, None),
            P(),
            P(),
            P(),
            P("branch", None),
            P("branch", None, SEQ, "fsdp"),
            P("branch", "fsdp", SEQ),
        ),
        out_specs=(P(SEQ, ("branch", "fsdp")), P(SEQ, ("branch", "fsdp"))),
        check_vma=False,
    )
```

profile of v0, /device:TPU:7, one launch (start us, length us, event | category | flops | bytes accessed | tf_op | source)
XLA Modules:
  0.0 498.1 jit_solution(12419808660584016517)
XLA Ops:
  7.2 0.0 copy-start
  7.2 0.0 copy-start.3
  7.2 0.0 copy-start.6
  7.2 0.0 all-gather.9.cloned.1.call-start
  7.2 0.7 all-gather.9.cloned.1.call-update
  7.9 0.0 all-gather.7.cloned.1.call-start
  8.0 1.3 fusion.53
  10.7 0.0 copy-start.2
  10.7 1.4 fusion.52
  12.1 4.8 multiply_reduce_fusion.1
  16.9 0.0 copy-done
  16.9 0.9 fusion.38
  17.8 0.9 fusion.40
  18.7 3.5 fusion.13
  22.2 161.2 %all-gather.9.cloned.1.call-done = bf16[1,3,5120,384]{3,2,1,0:T(8,128)(2,1)} async-done(((bf16[1,3,320,384]{3,2,1,0:T(8,128)(2,1)}), bf16[1,3,5120,384]{3,2,1,0:T(8,128)(2,1)}) %all-gather.9.cloned.1.call-update) | async-done | bytes 11796496 | tf_op jit(solution)/shard_map/all_gather | solution.py:125
  183.4 10.5 %fusion.18 = bf16[2,3,192,384]{3,2,1,0:T(8,128)(2,1)S(1)} fusion(bf16[1,3,5120,384]{3,2,1,0:T(8,128)(2,1)} %all-gather.9.cloned.1.call-done, bf16[1,192,5120]{2,1,0:T(8,128)(2,1)} %get-tuple-element.7, bf16[1,192,5120]{2,1,0:T(8,128)(2,1)} %get-tuple-element.6), kind=kOutput, calls=%fused_computation.26 | convolution fusion | flops 4538155008 | bytes 16613376 | tf_op jit(solution)/shard_map/ptd,jdc->pjtc/dot_general | solution.py:122
  193.9 0.1 fusion.51
  194.0 0.9 pad_maximum_fusion
  194.9 0.0 all-gather.7.cloned.1.call-update
  194.9 0.0 all-gather.11.cloned.1.call-start
  194.9 0.0 copy-done.5
  195.0 8.8 %all-gather.1 = bf16[1,384,640]{1,2,0:T(8,128)(2,1)} all-gather(bf16[1,384,320]{1,2,0:T(8,128)(2,1)S(1)} %copy-done.5), channel_id=3, replica_groups=mesh['branch'=2,'seq_0'=8,'seq_1'=2,'fsdp'=8] {'seq_1'}, dimensions={2}, use_global_device_ids=true | all-gather | bytes 737280 | tf_op jit(solution)/shard_map/all_gather | solution.py:18
  203.8 0.0 all-gather.11.cloned.1.call-update
  203.8 0.1 reshape_squeeze.3
  203.9 134.3 %all-gather.7.cloned.1.call-done = bf16[4,3072,384]{2,1,0:T(8,128)(2,1)} async-done(((bf16[4,192,384]{2,1,0:T(8,128)(2,1)}), bf16[4,3072,384]{2,1,0:T(8,128)(2,1)}) %all-gather.7.cloned.1.call-update) | async-done | bytes 9437200 | tf_op jit(solution)/shard_map/all_gather | solution.py:28
  338.2 8.4 %fusion.50 = (bf16[2,3072,384]{2,1,0:T(8,128)(2,1)}, bf16[2,3072,384]{2,1,0:T(8,128)(2,1)}) fusion(bf16[4,3072,384]{2,1,0:T(8,128)(2,1)} %all-gather.7.cloned.1.call-done), kind=kLoop, calls=%fused_computation.66 | loop fusion | bytes 18874368 | tf_op jit(solution)/shard_map/split | solution.py:28
  346.6 6.7 %copy.24 = bf16[2,3072,384]{1,2,0:T(8,128)(2,1)} copy(bf16[2,3072,384]{2,1,0:T(8,128)(2,1)} %get-tuple-element.4) | data formatting | bytes 9437184 | tf_op jit(solution)/shard_map/split | solution.py:28
  353.2 6.6 %copy.23 = bf16[2,3072,384]{1,2,0:T(8,128)(2,1)} copy(bf16[2,3072,384]{2,1,0:T(8,128)(2,1)} %get-tuple-element.5) | data formatting | bytes 9437184 | tf_op jit(solution)/shard_map/split | solution.py:28
  359.8 9.5 %bitcast_reduce_fusion = (f32[2,192,3]{1,2,0:T(4,128)S(1)}, f32[2,3,3072,192]{2,3,1,0:T(8,128)}) fusion(bf16[2,3072,3,128]{1,3,2,0:T(8,128)(2,1)} %bitcast.119, bf16[2,192,3,128]{3,2,1,0:T(4,128)(2,1)S(1)} %reshape_squeeze.3), kind=kOutput, calls=%fused_computation.1 | convolution fusion | flops 913046400 | bytes 19173888 | tf_op jit(solution)/shard_map/pqhd,prhd->pqhr/dot_general | solution.py:83
  369.3 7.7 %fusion.3 = f32[2,192,3]{1,2,0:T(4,128)S(1)} fusion(f32[2,3,3072,192]{2,3,1,0:T(8,128)} %get-tuple-element.20, f32[2,192,3]{1,2,0:T(4,128)S(1)} %broadcast_maximum_fusion), kind=kLoop, calls=%fused_computation.5 | loop fusion | flops 10615680 | bytes 14164992 | tf_op jit(solution)/shard_map/reduce_sum | solution.py:88
  377.1 7.9 %fusion.27 = bf16[2,192,3,128]{3,1,2,0:T(8,128)(2,1)S(1)} fusion(bf16[2,3072,3,128]{1,3,2,0:T(8,128)(2,1)S(1)} %bitcast.121, f32[2,3,3072,192]{2,3,1,0:T(8,128)} %get-tuple-element.20, f32[2,192,3]{1,2,0:T(4,128)S(1)} %broadcast_maximum_fusion, f32[2,192,3]{1,2,0:T(4,128)S(1)} %fusion.3), kind=kOutput, calls=%fused_computation.29 | convolution fusion | flops 916881408 | bytes 19178496 | tf_op jit(solution)/shard_map/pqhr,prhd->pqhd/dot_general | solution.py:89
  384.9 0.3 copy.28
  385.2 0.3 reshape.81
  385.5 4.1 all-gather.11.cloned.1.call-done
  389.6 6.8 %convert_bitcast_fusion = bf16[2,192,8,2,320]{4,1,2,3,0:T(8,128)(2,1)} fusion(bf16[2,8,320,384,1]{3,2,1,0,4:T(8,128)(2,1)} %bitcast.122, bf16[2,192,384,1,1]{2,1,0,3,4:T(8,128)(2,1)S(1)} %reshape.81), kind=kOutput, calls=%fused_computation.13 | convolution fusion | flops 1511915520 | bytes 8159232 | tf_op jit(solution)/shard_map/ptc,cd->ptd/dot_general | solution.py:137
  396.4 9.4 %copy.29 = bf16[2,192,8,2,320]{4,3,2,1,0:T(2,128)(2,1)} copy(bf16[2,192,8,2,320]{4,1,2,3,0:T(8,128)(2,1)} %convert_bitcast_fusion) | data formatting | bytes 7864320 | tf_op jit(solution)/shard_map/convert_element_type | solution.py:145
  405.8 10.0 %convert_element_type.88 = bf16[2,192,8,640]{3,2,1,0:T(8,128)(2,1)} reshape(bf16[2,192,8,2,320]{4,3,2,1,0:T(2,128)(2,1)} %copy.29) | data formatting | bytes 7864320 | tf_op jit(solution)/shard_map/convert_element_type | solution.py:145
  415.8 4.6 copy.30
  420.4 5.2 %all-to-all-start = ((bf16[8,2,192,640]{3,2,1,0:T(8,128)(2,1)}), bf16[8,2,192,640]{3,2,1,0:T(8,128)(2,1)}, u32[]{:S(2)}, u32[]{:S(2)}) async-start(bf16[8,2,192,640]{3,2,1,0:T(8,128)(2,1)} %copy.30), calls=%async_computation | async-start | bytes 7864320 | tf_op jit(solution)/shard_map/all_to_all | solution.py:38
  425.5 56.6 %all-to-all-done = bf16[8,2,192,640]{3,2,1,0:T(8,128)(2,1)} async-done(((bf16[8,2,192,640]{3,2,1,0:T(8,128)(2,1)}), bf16[8,2,192,640]{3,2,1,0:T(8,128)(2,1)}, u32[]{:S(2)}, u32[]{:S(2)}) %all-to-all-start) | async-done | bytes 3932192 | tf_op jit(solution)/shard_map/all_to_all | solution.py:38
  482.1 2.8 convert_reduce_fusion
  484.9 0.2 dynamic-slice_convert_fusion
  485.0 0.7 slice_bitcast_fusion.2
  485.8 1.9 collective-permute-start
  487.7 0.0 collective-permute-start.1
  487.7 1.2 collective-permute-done
  488.9 0.5 collective-permute-done.1
  489.4 2.1 fusion.34
  (12 shorter events, 0.0 us)
Async XLA Ops:
  7.2 9.8 %copy-start = (f32[16,5120]{1,0:T(8,128)S(1)}, f32[16,5120]{1,0:T(8,128)}, u32[]{:S(2)}) copy-start(f32[16,5120]{1,0:T(8,128)} %param.12) | copy-start | bytes 983044
  7.2 11.5 %copy-start.3 = (bf16[192,5120]{1,0:T(8,128)(2,1)S(1)}, bf16[192,5120]{1,0:T(8,128)(2,1)}, u32[]{:S(2)}) copy-start(bf16[192,5120]{1,0:T(8,128)(2,1)} %param.8) | copy-start | bytes 5898244
  7.2 11.5 %copy-start.6 = (f32[1,5120]{1,0:T(1,128)S(1)}, f32[1,5120]{1,0:T(1,128)}, u32[]{:S(2)}) copy-start(f32[1,5120]{1,0:T(1,128)} %param.13) | copy-start | bytes 61444
  7.2 176.2 %all-gather.9.cloned.1.call-start = ((), (), s32[]{:S(2)}) async-start(), calls=%async_computation.2 | async-start | bytes 12533760 | tf_op jit(solution)/shard_map/all_gather | solution.py:125
  7.9 330.3 %all-gather.7.cloned.1.call-start = ((), (), s32[]{:S(2)}) async-start(), calls=%async_computation.1 | async-start | bytes 10027008 | tf_op jit(solution)/shard_map/all_gather | solution.py:28
  10.7 8.0 %copy-start.2 = (bf16[2,192,5120]{2,1,0:T(8,128)(2,1)S(1)}, bf16[2,192,5120]{2,1,0:T(8,128)(2,1)}, u32[]{:S(2)}) copy-start(bf16[2,192,5120]{2,1,0:T(8,128)(2,1)} %param.9) | copy-start | bytes 11796484
  183.4 11.5 %copy-start.5 = (bf16[1,384,320]{1,2,0:T(8,128)(2,1)S(1)}, bf16[1,384,320]{1,2,0:T(8,128)(2,1)}, u32[]{:S(2)}) copy-start(bf16[1,384,320]{1,2,0:T(8,128)(2,1)} %param.15) | copy-start | bytes 737284
  194.9 194.7 %all-gather.11.cloned.1.call-start = ((), (), s32[]{:S(2)}) async-start(), calls=%async_computation.3 | async-start | bytes 4423680 | tf_op jit(solution)/shard_map/all_gather | solution.py:18
  369.3 7.7 %copy-start.4 = (bf16[2,3072,384]{1,2,0:T(8,128)(2,1)S(1)}, bf16[2,3072,384]{1,2,0:T(8,128)(2,1)}, u32[]{:S(2)}) copy-start(bf16[2,3072,384]{1,2,0:T(8,128)(2,1)} %copy.23) | copy-start | bytes 14155780
  420.4 61.7 %all-to-all-start = ((bf16[8,2,192,640]{3,2,1,0:T(8,128)(2,1)}), bf16[8,2,192,640]{3,2,1,0:T(8,128)(2,1)}, u32[]{:S(2)}, u32[]{:S(2)}) async-start(bf16[8,2,192,640]{3,2,1,0:T(8,128)(2,1)} %copy.30), calls=%async_computation | async-start | bytes 7864320 | tf_op jit(solution)/shard_map/all_to_all | solution.py:38
  425.5 63.9 %slice-start = ((bf16[2,192,5120]{2,1,0:T(8,128)(2,1)}), bf16[1,192,5120]{2,1,0:T(8,128)(2,1)S(1)}, s32[]{:S(2)}) async-start(bf16[2,192,5120]{2,1,0:T(8,128)(2,1)} %param.9), calls=%async_computation.4 | async-start | bytes 3932160 | tf_op jit(solution)/shard_map/slice | solution.py:160
  482.1 9.4 %copy-start.1 = (f32[16,5120]{1,0:T(8,128)S(1)}, f32[16,5120]{1,0:T(8,128)}, u32[]{:S(2)}) copy-start(f32[16,5120]{1,0:T(8,128)} %param.12) | copy-start | bytes 983044
  485.8 3.1 collective-permute-start
  487.7 1.7 collective-permute-start.1
Sparse Core Ops, SparseCore 0:
  10.6 172.7 all-gather.8
  195.0 143.1 all-gather.6
  340.0 49.5 all-gather.10
where the time goes:
time: 499 us; the launch traced here: 498 us
  waiting for transfers between devices  359 us (72%)
  local copies, waits for them, and re-layouts  50 us (10%)
  matrix products  36.4 us (7%)
  other arithmetic  21.8 us (4%)
  between operations  15.3 us (3%)
  blocking collectives  8.79 us (2%)
  starting transfers between devices  7.2 us (1%)
    all_gather x1, waiting for transfers between devices, body(): lax.all_gather(weights, SEQ, axis=1, tiled=True)  161 us
    all_gather x1, waiting for transfers between devices, sent_together(): lax.all_gather(both, axis, axis=dim, tiled=True)  134 us
    all_to_all x1, waiting for transfers between devices, sent_and_summed(): blocks = lax.all_to_all(in_blocks(x, dim, count), axis, 0, 0, tiled=True)  56.6 us
    split x3, local copies, waits for them, and re-layouts, sent_together(): jnp.split(lax.all_gather(both, axis, axis=dim, tiled=True), ends, axis=al...  21.6 us
    convert_element_type x2, local copies, waits for them, and re-layouts, body(): head_sums = sent_and_summed(partial_value.astype(jnp.bfloat16), 'fsdp', 2)  19.4 us
    dot_general x1, matrix products, body(): jnp.einsum('ptd,jdc->pjtc', inputs, lax.all_gather(weights, SEQ, axis=1,...  10.5 us
  transfers between devices with their start and end apart: 6, of which 6 were waited for; matrix products, arithmetic and copies ran while one was open for 12% of the time, Pallas kernels for 0%

commit v1 on v0

v1 whole, which is shorter than its diff:
```python
import functools

import jax
import jax.numpy as jnp
from jax import lax
from jax.experimental import pallas as pl
from jax.experimental.pallas import tpu as pltpu
from jax.sharding import Mesh
from jax.sharding import PartitionSpec as P

HD = 128
GUIDANCE = 3.5
EPSILON = 1e-06
MESH = pl.DeviceIdType.MESH
BF16, F32 = jnp.bfloat16, jnp.float32

AXES = ("core", "z", "y_hi", "y_lo", "x")
NZ = 8
TOK = 192
DZ = 640
ROWS = 320
COLS = 384
UNITS = 6
RB = 16


def sigma_of(step_index):
    fraction = step_index.astype(F32) / 1000.0
    return 5.0 * fraction / (1.0 + 4.0 * fraction)


def owner_of(unit):
    return unit + unit // 3


def attend_kernel(
    coef, lat_hbm, noise_hbm, shift, gain, w_hbm, out,
    lat, noi, hb, inv, wbuf, acc, units, ub, ob,
    s_in, s_w, r_w, s_h, r_h, s_ring, r_ring, s_sib, r_sib, s_a, r_a, s_kv, r_kv, s_o, r_o,
):
    core, z, y_hi = lax.axis_index("core"), lax.axis_index("z"), lax.axis_index("y_hi")
    swapped = core != y_hi
    sel = lax.rem(core + y_hi, 2)
    partner = {"core": 1 - core, "y_hi": 1 - y_hi}
    sibling = {"core": 1 - core}

    def at_z(step):
        return lax.rem(z + step + NZ, NZ)

    def remote(src, dst, send, recv, device):
        return pltpu.make_async_remote_copy(
            src_ref=src, dst_ref=dst, send_sem=send, recv_sem=recv, device_id=device, device_id_type=MESH
        )

    loads = [
        pltpu.make_async_copy(lat_hbm, lat, s_in.at[0]),
        pltpu.make_async_copy(noise_hbm.at[0], noi.at[0], s_in.at[1]),
        pltpu.make_async_copy(noise_hbm.at[core], noi.at[1], s_in.at[2]),
    ]
    for load in loads:
        load.start()

    barrier = pltpu.get_barrier_semaphore()
    pl.semaphore_signal(barrier, inc=1, device_id=partner, device_id_type=MESH)
    pl.semaphore_signal(barrier, inc=1, device_id=sibling, device_id_type=MESH)
    for step in range(1, NZ):
        pl.semaphore_signal(barrier, inc=1, device_id={"z": at_z(step)}, device_id_type=MESH)
    pl.semaphore_wait(barrier, NZ + 1)

    my_rows = pl.ds(core * ROWS, ROWS)
    sib_rows = pl.ds((1 - core) * ROWS, ROWS)

    def own_local(j):
        return pltpu.make_async_copy(w_hbm.at[j], wbuf.at[z, j, my_rows], r_w.at[j])

    def own_remote(j):
        return remote(
            w_hbm.at[j], wbuf.at[z, j, pl.ds(y_hi * ROWS, ROWS)], s_w.at[j], r_w.at[j], partner
        )

    @pl.when(swapped)
    def _():
        for j in range(3):
            own_remote(j).start()

    @pl.when(jnp.logical_not(swapped))
    def _():
        for j in range(3):
            own_local(j).start()

    def ring(direction, k, j):
        sign = 1 - 2 * direction
        slot = at_z(-sign * (k - 1))
        if k < 4:
            rows = my_rows
        else:
            rows = pl.ds(core * ROWS + direction * (ROWS // 2), ROWS // 2)
        block = wbuf.at[slot, j, rows]
        return remote(
            block, block, s_ring.at[direction, k - 1, j], r_ring.at[direction, k - 1, j], {"z": at_z(sign)}
        )

    def landing(direction, k, j):
        sign = 1 - 2 * direction
        slot = at_z(-sign * k)
        if k < 4:
            rows = my_rows
        else:
            rows = pl.ds(core * ROWS + direction * (ROWS // 2), ROWS // 2)
        block = wbuf.at[slot, j, rows]
        return remote(
            block, block, s_ring.at[direction, k - 1, j], r_ring.at[direction, k - 1, j], {"z": at_z(sign)}
        )

    def to_sibling(index, slot, j):
        block = wbuf.at[slot, j, my_rows]
        return remote(block, block, s_sib.at[index, j], r_sib.at[index, j], sibling)

    def from_sibling(index, slot, j):
        block = wbuf.at[slot, j, sib_rows]
        return remote(block, block, s_sib.at[index, j], r_sib.at[index, j], sibling)

    def begin_ring():
        for j in range(3):
            own_local(j).wait()
            ring(0, 1, j).start()
            ring(1, 1, j).start()
            to_sibling(0, z, j).start()

    pl.when(jnp.logical_not(swapped))(begin_ring)

    for load in loads:
        load.wait()

    def mixed(p, rows, cols):
        return coef[p, 0] * lat[rows, cols].astype(F32) + coef[p, 1] * noi[p, rows, cols].astype(F32)

    for p in range(2):

        @pl.loop(0, TOK // RB)
        def _(b, p=p):
            rows = pl.ds(pl.multiple_of(b * RB, RB), RB)
            total = jnp.zeros((RB, DZ), F32)
            for q in range(NZ):
                part = mixed(p, rows, pl.ds(q * DZ, DZ))
                total = total + part * part
            mean = jnp.sum(total, axis=1, keepdims=True) * (1.0 / (NZ * DZ))
            inv[p, rows, :] = lax.rsqrt(mean + EPSILON)

    def h_copy(slot):
        return remote(hb.at[0, slot], hb.at[1, slot], s_h.at[slot], r_h.at[slot], partner)

    def distance(i):
        return lax.rem(i + 1, 2) * (-((i + 1) // 2)) + lax.rem(i, 2) * ((i + 1) // 2)

    @pl.loop(0, NZ)
    def _(i):
        slot = at_z(distance(i))
        cols = pl.ds(pl.multiple_of(slot * DZ, 128), DZ)
        for p in range(2):

            @pl.loop(0, TOK // RB)
            def _(b, p=p):
                start = pl.multiple_of(b * RB, RB)
                rows = pl.ds(start, RB)
                part = mixed(p, rows, cols) * inv[p, rows, :] * gain[:, cols] + shift[p : p + 1, cols]
                hb[0, slot, pl.ds(p * TOK + start, RB), :] = part.astype(BF16)

        @pl.when(swapped)
        def _():
            h_copy(slot).start()

    pl.when(swapped)(begin_ring)

    acc[...] = jnp.zeros_like(acc)

    def multiply(index, slot):
        for j in range(3):
            from_sibling(index, slot, j).wait_recv()

        @pl.when(swapped)
        def _():
            h_copy(slot).wait_recv()

        @pl.loop(0, 3)
        def _(j):
            acc[j] += jnp.dot(hb[sel, slot], wbuf[slot, j], preferred_element_type=F32)

    groups = [[(0, 0)], [(1, -1), (2, 1)], [(3, -2), (4, 2)], [(5, -3), (6, 3)], [(7, 4)]]
    for k in range(1, 5):
        for j in range(3):
            for direction in range(2):
                landing(direction, k, j).wait_recv()
                if k < 4:
                    ring(direction, k + 1, j).start()
                    index, step = groups[k][direction]
                    to_sibling(index, at_z(step), j).start()
            if k == 4:
                index, step = groups[k][0]
                to_sibling(index, at_z(step), j).start()
        for index, step in groups[k - 1]:
            multiply(index, at_z(step))
    for index, step in groups[4]:
        multiply(index, at_z(step))

    my_part = pl.ds(z * TOK, TOK)

    def unit_remote(u):
        return remote(
            units.at[u], ub.at[:, core, my_part], s_a.at[u], r_a.at[z], {"z": owner_of(u)}
        )

    def unit_local(u):
        return pltpu.make_async_copy(units.at[u], ub.at[:, core, my_part], r_a.at[z])

    for u in range(UNITS):
        p, h = u // 3, u % 3
        for j in range(3):
            units[u, j] = acc[j, p * TOK : (p + 1) * TOK, h * HD : (h + 1) * HD].astype(BF16)

        @pl.when(z == owner_of(u))
        def _(u=u):
            unit_local(u).start()

        @pl.when(z != owner_of(u))
        def _(u=u):
            unit_remote(u).start()

    is_owner = lax.rem(z, 4) != 3
    mine = jnp.minimum(z - z // 4, UNITS - 1)

    def arrived(source):
        block = ub.at[:, core, pl.ds(source * TOK, TOK)]
        return remote(block, block, s_a.at[0], r_a.at[source], sibling)

    def kv_to_sibling(source, which):
        block = ub.at[pl.ds(1, 2), which, pl.ds(source * TOK, TOK)]
        return remote(block, block, s_kv.at[source], r_kv.at[source], sibling)

    def o_remote(to):
        return remote(ob.at[to], out.at[mine], s_o.at[to], r_o.at[mine], {"z": to})

    def o_local(to):
        return pltpu.make_async_copy(ob.at[to], out.at[mine], r_o.at[mine])

    @pl.when(is_owner)
    def _():
        @pl.loop(0, NZ)
        def _(i):
            source = at_z(distance(i))
            arrived(source).wait_recv()
            kv_to_sibling(source, core).start()

        @pl.loop(0, NZ)
        def _(i):
            kv_to_sibling(at_z(distance(i)), 1 - core).wait_recv()

        @pl.loop(0, NZ)
        def _(i):
            to = at_z(distance(NZ - 1 - i))
            queries = ub[0, core, pl.ds(pl.multiple_of(to * TOK, TOK), TOK), :]
            keys = ub[1].reshape(2 * NZ * TOK, HD)
            scores = lax.dot_general(
                queries, keys, (((1,), (1,)), ((), ())), preferred_element_type=F32
            ) * (HD**-0.5)
            peak = jnp.max(scores, axis=1, keepdims=True)
            weight = jnp.exp(scores - peak)
            mass = jnp.sum(weight, axis=1, keepdims=True)
            result = jnp.dot(
                weight.astype(BF16), ub[2].reshape(2 * NZ * TOK, HD), preferred_element_type=F32
            )
            ob[to] = (result / mass).astype(BF16)

            @pl.when(to == z)
            def _():
                o_local(to).start()

            @pl.when(to != z)
            def _():
                o_remote(to).start()

    for u in range(UNITS):
        block = out.at[u]
        remote(block, block, s_o.at[0], r_o.at[u], sibling).wait_recv()

    @pl.when(swapped)
    def _():
        for j in range(3):
            own_remote(j).wait_send()
        for slot in range(NZ):
            h_copy(slot).wait_send()

    for k in range(1, 5):
        for j in range(3):
            for direction in range(2):
                ring(direction, k, j).wait_send()
    for group in groups:
        for index, step in group:
            for j in range(3):
                to_sibling(index, at_z(step), j).wait_send()
    for u in range(UNITS):

        @pl.when(z != owner_of(u))
        def _(u=u):
            unit_remote(u).wait_send()

    @pl.when(is_owner)
    def _():
        for source in range(NZ):
            kv_to_sibling(source, core).wait_send()

            @pl.when(z != source)
            def _(source=source):
                o_remote(source).wait_send()


def attend(coef, latents, noise, shift, gain, w_qkv):
    dma = pltpu.SemaphoreType.DMA
    vmem, any_space = pl.BlockSpec(memory_space=pltpu.VMEM), pl.BlockSpec(memory_space=pl.ANY)
    return pl.pallas_call(
        attend_kernel,
        out_shape=jax.ShapeDtypeStruct((UNITS, TOK, HD), BF16),
        in_specs=[pl.BlockSpec(memory_space=pltpu.SMEM), any_space, any_space, vmem, vmem, any_space],
        out_specs=vmem,
        scratch_shapes=[
            pltpu.VMEM((TOK, NZ * DZ), BF16),
            pltpu.VMEM((2, TOK, NZ * DZ), BF16),
            pltpu.VMEM((2, NZ, 2 * TOK, DZ), BF16),
            pltpu.VMEM((2, TOK, 1), F32),
            pltpu.VMEM((NZ, 3, DZ, COLS), BF16),
            pltpu.VMEM((3, 2 * TOK, COLS), F32),
            pltpu.VMEM((UNITS, 3, TOK, HD), BF16),
            pltpu.VMEM((3, 2, NZ * TOK, HD), BF16),
            pltpu.VMEM((NZ, TOK, HD), BF16),
            dma((3,)),
            dma((3,)), dma((3,)),
            dma((NZ,)), dma((NZ,)),
            dma((2, 4, 3)), dma((2, 4, 3)),
            dma((NZ, 3)), dma((NZ, 3)),
            dma((UNITS,)), dma((NZ,)),
            dma((NZ,)), dma((NZ,)),
            dma((NZ,)), dma((UNITS,)),
        ],
        compiler_params=pltpu.CompilerParams(
            collective_id=0, has_side_effects=True, vmem_limit_bytes=58 * 2**20
        ),
        cost_estimate=pl.CostEstimate(
            flops=9_000_000_000, bytes_accessed=40_000_000, transcendentals=5_000_000
        ),
    )(coef, latents, noise, shift, gain, w_qkv)


def body(latents, noise, time_index, cfg_pair, cond_table, gain, w_qkv, w_out):
    core = lax.axis_index("core")
    levels = sigma_of(time_index)
    level = jnp.stack([levels[0], levels[core]])
    coef = jnp.stack([1.0 - level, level], axis=1)
    second = cfg_pair[1 - core]
    shift = jnp.concatenate(
        [
            lax.dynamic_slice_in_dim(cond_table, cfg_pair[0], 1, 0),
            lax.dynamic_slice_in_dim(cond_table, second, 1, 0),
        ]
    )
    attn = attend(coef, latents, noise, shift, gain, w_qkv[0])
    attn = attn.reshape(2, 3, TOK, HD).transpose(0, 2, 1, 3).reshape(2, TOK, COLS)

    across = ("core", "y_hi")
    w_own = lax.ppermute(w_out[0], across, [(0, 0), (1, 2), (2, 1), (3, 3)])
    out_full = lax.all_gather(lax.all_gather(w_own, "core", axis=1, tiled=True), "z", axis=1, tiled=True)
    partial_value = jnp.einsum("ptc,cd->ptd", attn, out_full, preferred_element_type=F32).astype(BF16)
    blocks = partial_value.reshape(2, TOK, 2, 8, ROWS).transpose(3, 2, 0, 1, 4)
    blocks = lax.all_to_all(blocks, ("y_lo", "x"), 0, 0, tiled=True)
    sums = jnp.sum(blocks.astype(F32), axis=0).astype(BF16)
    y_hi = lax.axis_index("y_hi")
    own = lax.ppermute(sums[y_hi], across, [(0, 0), (1, 2), (2, 1), (3, 3)]).astype(F32)
    other = lax.ppermute(sums[1 - y_hi], across, [(0, 2), (1, 0), (2, 3), (3, 1)]).astype(F32)
    is_teacher = core == 0
    teacher = jnp.where(is_teacher, own, other)
    critic = jnp.where(is_teacher, other, own)
    dmd_grad = critic[0] - (teacher[1] + GUIDANCE * (teacher[0] - teacher[1]))
    col_start = (core * 8 + lax.axis_index("y_lo") * 4 + lax.axis_index("x")) * ROWS
    noise_cols = lax.dynamic_slice_in_dim(noise[1], col_start, ROWS, 1).astype(F32)
    latent_cols = lax.dynamic_slice_in_dim(latents, col_start, ROWS, 1).astype(F32)
    return dmd_grad, critic[1] - (noise_cols - latent_cols)


def solution(mesh):
    torus = Mesh(mesh.devices.reshape(2, NZ, 2, 2, 4), AXES)
    seq, fsdp = ("z", "y_hi"), ("y_lo", "x")
    return jax.shard_map(
        body,
        mesh=torus,
        in_specs=(
            P(seq, None),
            P(None, seq, None),
            P(),
            P(),
            P(),
            P("core", None),
            P("core", None, seq, fsdp),
            P("core", fsdp, seq),
        ),
        out_specs=(P(seq, ("core", *fsdp)), P(seq, ("core", *fsdp))),
        check_vma=False,
    )
```

time: 499 us -> 306 us (0.61)
  waiting for transfers between devices: 359 us -> 78.1 us
  Pallas kernels: 0 us -> 145 us
  matrix products: 36.4 us -> 6.26 us
  local copies, waits for them, and re-layouts: 50 us -> 24.3 us
  starting transfers between devices: 7.2 us -> 17.8 us
  other arithmetic: 21.8 us -> 14.1 us
  blocking collectives: 8.79 us -> 2.15 us
    all_gather x3 -> x1, waiting for transfers between devices: 300 us -> 0.02 us  [body(): lax.all_gather(lax.all_gather(w_own, 'core', axis=1, tiled=True), 'z', ax...]
    pallas_call x0 -> x1, Pallas kernels: none -> 145 us  [attend(): pl.pallas_call(attend_kernel, out_shape=jax.ShapeDtypeStruct((UNITS, TOK,...]
    dot_general x6 -> x1, matrix products: 36.4 us -> 6.26 us  [body(): jnp.einsum('ptc,cd->ptd', attn, out_full, preferred_element_type=F32)]
    split x3 -> x0, local copies, waits for them, and re-layouts: 21.6 us -> none  [sent_together(): jnp.split(lax.all_gather(both, axis, axis=dim, tiled=True), ends, axis=al...]
    convert_element_type x4 -> x0, local copies, waits for them, and re-layouts: 20.4 us -> none  [the longest x2 19.4 us: body(): head_sums = sent_and_summed(partial_value.astype(jnp.bfloat16), 'fsdp', 2)]
    reshape x1 -> x4, local copies, waits for them, and re-layouts: 0.25 us -> 18.9 us  [the longest x2 17.4 us: body(): blocks = partial_value.reshape(2, TOK, 2, 8, ROWS).transpose(3, 2, 0, 1, 4)]
    all_to_all x1, waiting for transfers between devices: 56.6 us -> 68.3 us  [body(): blocks = lax.all_to_all(blocks, ('y_lo', 'x'), 0, 0, tiled=True)]
    ppermute x2 -> x3, starting transfers between devices: 1.92 us -> 12.6 us  [the longest x1 5.38 us: body(): w_own = lax.ppermute(w_out[0], across, [(0, 0), (1, 2), (2, 1), (3, 3)])]
  transfers between devices with their start and end apart: 6 -> 5, of which waited for: 6 -> 3; matrix products, arithmetic and copies ran while one was open for 12% -> 3% of each run, Pallas kernels for 0% -> 47%
where the time goes in v1:
time: 306 us; the launch traced here: 305 us
  Pallas kernels  145 us (47%)
  waiting for transfers between devices  78.1 us (26%)
  local copies, waits for them, and re-layouts  24.3 us (8%)
  between operations  18 us (6%)
  starting transfers between devices  17.8 us (6%)
  other arithmetic  14.1 us (5%)
  matrix products  6.26 us (2%)
    pallas_call x1, Pallas kernels, attend(): pl.pallas_call(attend_kernel, out_shape=jax.ShapeDtypeStruct((UNITS, TOK,...  145 us
    all_to_all x1, waiting for transfers between devices, body(): blocks = lax.all_to_all(blocks, ('y_lo', 'x'), 0, 0, tiled=True)  68.3 us
    reshape x2, local copies, waits for them, and re-layouts, body(): blocks = partial_value.reshape(2, TOK, 2, 8, ROWS).transpose(3, 2, 0, 1, 4)  17.4 us
    reduce_sum x1, other arithmetic, body(): sums = jnp.sum(blocks.astype(F32), axis=0).astype(BF16)  7.48 us
    dot_general x1, matrix products, body(): jnp.einsum('ptc,cd->ptd', attn, out_full, preferred_element_type=F32)  6.26 us
  transfers between devices with their start and end apart: 5, of which 3 were waited for; matrix products, arithmetic and copies ran while one was open for 3% of the time, Pallas kernels for 47%

profile of v1, /device:TPU:7, one launch (start us, length us, event | category | flops | bytes accessed | tf_op | source)
XLA Modules:
  0.0 305.3 jit_solution(12792507810635722280)
XLA Ops:
  7.2 0.0 all-gather.2.cloned.1.call-start
  7.2 5.4 %collective-permute-start = (bf16[384,320]{0,1:T(8,128)(2,1)}, bf16[384,320]{0,1:T(8,128)(2,1)S(1)}, u32[]{:S(2)}, u32[]{:S(2)}) collective-permute-start(bf16[384,320]{0,1:T(8,128)(2,1)} %bitcast.56), channel_id=1, source_target_pairs={{0,0},{8,128},{128,8},{136,136},{1,1},{9,129},{129,9},{137,137},{2... | collective-permute-start | bytes 737288 | tf_op jit(solution)/shard_map/ppermute | solution.py:369
  12.6 4.1 %collective-permute-done = bf16[384,320]{0,1:T(8,128)(2,1)S(1)} collective-permute-done((bf16[384,320]{0,1:T(8,128)(2,1)}, bf16[384,320]{0,1:T(8,128)(2,1)S(1)}, u32[]{:S(2)}, u32[]{:S(2)}) %collective-permute-start) | collective-permute-done | bytes 245792 | tf_op jit(solution)/shard_map/ppermute | solution.py:369
  16.7 2.1 all_gather.6
  18.8 1.0 copy.23
  19.8 0.0 all-gather.2.cloned.1.call-update
  19.8 1.3 fusion.6
  23.7 0.7 add_divide_fusion
  24.4 0.6 fusion.7
  25.0 1.4 maximum_bitcast_fusion
  26.3 0.1 copy.21
  27.7 1.3 maximum_subtract_fusion
  29.0 0.6 pad_maximum_fusion.1.coef
  29.7 1.0 constant_dynamic-slice_fusion.3
  30.7 0.7 pad_maximum_fusion.shift
  31.3 144.7 %shard_map.95 = bf16[6,192,128]{2,1,0:T(8,128)(2,1)} custom-call(f32[2,2]{1,0:T(2,128)} %pad_maximum_fusion.1.coef, bf16[192,5120]{1,0:T(8,128)(2,1)} %lat_hbm.1, bf16[2,192,5120]{2,1,0:T(8,128)(2,1)} %noise_hbm.1, f32[2,5120]{1,0:T(2,128)} %pad_maximum_fusion.shift, f32[1,5120]{1,0:T(1,128)} %gain.1, bf16[3,320,384]{2,1,0:T(8,128)(2,1)} %bitcast.55), custom_call_target="tpu_custom_call" | custom-call | flops 8999999488 | bytes 40000000 | tf_op jit(solution)/shard_map/pallas_call | solution.py:320
  176.0 1.2 copy.36
  177.3 0.3 reshape.46
  177.5 0.0 all-gather.2.cloned.1.call-done
  177.5 6.3 %convolution_convert_fusion = bf16[2,192,5120]{2,1,0:T(8,128)(2,1)} fusion(bf16[2,192,384]{2,1,0:T(8,128)(2,1)S(1)} %reshape.46, bf16[384,5120]{1,0:T(8,128)(2,1)} %all-gather.2.cloned.1.call-done), kind=kOutput, calls=%fused_computation | convolution fusion | flops 1511915520 | bytes 8159232 | tf_op jit(solution)/shard_map/ptc,cd->ptd/dot_general | solution.py:371
  183.8 8.4 %reshape.47 = bf16[2,192,2,8,320]{4,3,2,1,0:T(8,128)(2,1)} reshape(bf16[2,192,5120]{2,1,0:T(8,128)(2,1)} %convolution_convert_fusion) | data formatting | bytes 7864320 | tf_op jit(solution)/shard_map/reshape | solution.py:372
  192.2 9.1 %copy.35 = bf16[2,192,2,8,320]{4,2,1,0,3:T(2,128)(2,1)} copy(bf16[2,192,2,8,320]{4,3,2,1,0:T(8,128)(2,1)} %reshape.47) | data formatting | bytes 7864320 | tf_op jit(solution)/shard_map/reshape | solution.py:372
  201.2 5.1 %all-to-all-start = ((bf16[8,2,2,192,320]{4,1,3,2,0:T(2,128)(2,1)}), bf16[8,2,2,192,320]{4,1,3,2,0:T(2,128)(2,1)}, u32[]{:S(2)}, u32[]{:S(2)}) async-start(bf16[8,2,2,192,320]{4,1,3,2,0:T(2,128)(2,1)} %bitcast.50), calls=%async_computation | async-start | bytes 9437184 | tf_op jit(solution)/shard_map/all_to_all | solution.py:373
  206.4 68.3 %all-to-all-done = bf16[8,2,2,192,320]{4,1,3,2,0:T(2,128)(2,1)} async-done(((bf16[8,2,2,192,320]{4,1,3,2,0:T(2,128)(2,1)}), bf16[8,2,2,192,320]{4,1,3,2,0:T(2,128)(2,1)}, u32[]{:S(2)}, u32[]{:S(2)}) %all-to-all-start) | async-done | bytes 3932192 | tf_op jit(solution)/shard_map/all_to_all | solution.py:373
  274.7 7.5 %reduce_sum.12 = bf16[2,2,192,320]{3,0,2,1:T(2,128)(2,1)S(1)} reduce(bf16[8,2,2,192,320]{4,1,3,2,0:T(2,128)(2,1)} %all-to-all-done, bf16[]{:T(256)} %constant.43.clone.1), dimensions={0}, to_apply=%region_0.0 | reduce | flops 1720320 | bytes 4423682 | tf_op jit(solution)/shard_map/reduce_sum | solution.py:374
  282.2 1.2 constant_dynamic-slice_fusion.1
  283.4 0.0 slice-start
  283.5 3.4 %collective-permute-start.1 = (bf16[2,192,320]{2,1,0:T(8,128)(2,1)S(1)}, bf16[2,192,320]{2,1,0:T(8,128)(2,1)S(1)}, u32[]{:S(2)}, u32[]{:S(2)}) collective-permute-start(bf16[2,192,320]{2,1,0:T(8,128)(2,1)S(1)} %bitcast.52), channel_id=1, source_target_pairs={{0,128},{8,0},{128,136},{136,8},{1,129},{9,1},{129,137},{137,9},{2... | collective-permute-start | bytes 737288 | tf_op jit(solution)/shard_map/ppermute | solution.py:377
  286.9 3.8 %collective-permute-start.2 = (bf16[2,192,320]{2,1,0:T(8,128)(2,1)S(1)}, bf16[2,192,320]{2,1,0:T(8,128)(2,1)S(1)}, u32[]{:S(2)}, u32[]{:S(2)}) collective-permute-start(bf16[2,192,320]{2,1,0:T(8,128)(2,1)S(1)} %bitcast.53), channel_id=1, source_target_pairs={{0,0},{8,128},{128,8},{136,136},{1,1},{9,129},{129,9},{137,137},{2... | collective-permute-start | bytes 737288 | tf_op jit(solution)/shard_map/ppermute | solution.py:376
  290.7 0.0 collective-permute-done.1
  290.8 5.7 %collective-permute-done.2 = bf16[2,192,320]{2,1,0:T(8,128)(2,1)S(1)} collective-permute-done((bf16[2,192,320]{2,1,0:T(8,128)(2,1)S(1)}, bf16[2,192,320]{2,1,0:T(8,128)(2,1)S(1)}, u32[]{:S(2)}, u32[]{:S(2)}) %collective-permute-start.2) | collective-permute-done | bytes 245792 | tf_op jit(solution)/shard_map/ppermute | solution.py:376
  296.5 0.1 convert_select_fusion.1
  296.5 0.0 slice-done
  296.6 1.9 fusion.1
  (2 shorter events, 0.1 us)
Async XLA Ops:
  7.2 170.4 %all-gather.2.cloned.1.call-start = ((), (), s32[]{:S(2)}) async-start(), calls=%async_computation.1 | async-start | bytes 4423680 | tf_op jit(solution)/shard_map/all_gather | solution.py:370
  7.2 9.5 %collective-permute-start = (bf16[384,320]{0,1:T(8,128)(2,1)}, bf16[384,320]{0,1:T(8,128)(2,1)S(1)}, u32[]{:S(2)}, u32[]{:S(2)}) collective-permute-start(bf16[384,320]{0,1:T(8,128)(2,1)} %bitcast.56), channel_id=1, source_target_pairs={{0,0},{8,128},{128,8},{136,136},{1,1},{9,129},{129,9},{137,137},{2... | collective-permute-start | bytes 737288 | tf_op jit(solution)/shard_map/ppermute | solution.py:369
  201.2 73.5 %all-to-all-start = ((bf16[8,2,2,192,320]{4,1,3,2,0:T(2,128)(2,1)}), bf16[8,2,2,192,320]{4,1,3,2,0:T(2,128)(2,1)}, u32[]{:S(2)}, u32[]{:S(2)}) async-start(bf16[8,2,2,192,320]{4,1,3,2,0:T(2,128)(2,1)} %bitcast.50), calls=%async_computation | async-start | bytes 9437184 | tf_op jit(solution)/shard_map/all_to_all | solution.py:373
  283.4 13.1 %slice-start = ((bf16[2,192,5120]{2,1,0:T(8,128)(2,1)}), bf16[1,192,5120]{2,1,0:T(8,128)(2,1)S(1)}, s32[]{:S(2)}) async-start(bf16[2,192,5120]{2,1,0:T(8,128)(2,1)} %noise_hbm.1), calls=%async_computation.2 | async-start | bytes 3932160 | tf_op jit(solution)/shard_map/slice | solution.py:383
  283.5 7.3 %collective-permute-start.1 = (bf16[2,192,320]{2,1,0:T(8,128)(2,1)S(1)}, bf16[2,192,320]{2,1,0:T(8,128)(2,1)S(1)}, u32[]{:S(2)}, u32[]{:S(2)}) collective-permute-start(bf16[2,192,320]{2,1,0:T(8,128)(2,1)S(1)} %bitcast.52), channel_id=1, source_target_pairs={{0,128},{8,0},{128,136},{136,8},{1,129},{9,1},{129,137},{137,9},{2... | collective-permute-start | bytes 737288 | tf_op jit(solution)/shard_map/ppermute | solution.py:377
  286.9 9.5 %collective-permute-start.2 = (bf16[2,192,320]{2,1,0:T(8,128)(2,1)S(1)}, bf16[2,192,320]{2,1,0:T(8,128)(2,1)S(1)}, u32[]{:S(2)}, u32[]{:S(2)}) collective-permute-start(bf16[2,192,320]{2,1,0:T(8,128)(2,1)S(1)} %bitcast.53), channel_id=1, source_target_pairs={{0,0},{8,128},{128,8},{136,136},{1,1},{9,129},{129,9},{137,137},{2... | collective-permute-start | bytes 737288 | tf_op jit(solution)/shard_map/ppermute | solution.py:376
Sparse Core Ops, SparseCore 0:
  20.0 80.2 all-gather.1

commit v2 on v1

v2 whole, which is shorter than its diff:
```python
import functools

import jax
import jax.numpy as jnp
from jax import lax
from jax.experimental import pallas as pl
from jax.experimental.pallas import tpu as pltpu
from jax.sharding import Mesh
from jax.sharding import PartitionSpec as P

HD = 128
LOG2E = 1.4426950408889634
GUIDANCE = 3.5
EPSILON = 1e-06
MESH = pl.DeviceIdType.MESH
BF16, F32 = jnp.bfloat16, jnp.float32

AXES = ("core", "z", "y_hi", "y_lo", "x")
NZ = 8
TOK = 192
DZ = 640
ROWS = 320
COLS = 384
UNITS = 6
RB = 64


def owner_of(unit):
    return unit + unit // 3


def step_kernel(
    times, pair, lat_hbm, noise_hbm, cond, gain, w_hbm, wo_hbm, fin,
    lat, noi, shift, hb, inv, wbuf, acc, units, ub, ob, att, wo, pred, pb,
    s_in, s_w, r_w, s_h, r_h, s_ring, r_ring, s_sib, r_sib, s_a, r_a, s_kv, r_kv, s_o, r_o,
    s_wa, s_wo, r_wo, s_att, r_att, s_f, r_f,
):
    core, z, y_hi = lax.axis_index("core"), lax.axis_index("z"), lax.axis_index("y_hi")
    y_lo, x = lax.axis_index("y_lo"), lax.axis_index("x")
    f = y_lo * 4 + x
    swapped = core != y_hi
    sel = lax.rem(core + y_hi, 2)
    partner = {"core": 1 - core, "y_hi": 1 - y_hi}
    sibling = {"core": 1 - core}

    def at_z(step):
        return lax.rem(z + step + NZ, NZ)

    def at_f(step):
        return lax.rem(f + step, 8)

    def f_device(peer):
        return {"y_lo": peer // 4, "x": lax.rem(peer, 4)}

    def remote(src, dst, send, recv, device):
        return pltpu.make_async_remote_copy(
            src_ref=src, dst_ref=dst, send_sem=send, recv_sem=recv, device_id=device, device_id_type=MESH
        )

    loads = [
        pltpu.make_async_copy(lat_hbm, lat, s_in.at[0]),
        pltpu.make_async_copy(noise_hbm.at[0], noi.at[0], s_in.at[1]),
        pltpu.make_async_copy(noise_hbm.at[core], noi.at[1], s_in.at[2]),
    ]
    for load in loads:
        load.start()

    half_in = z // 4
    in_y_lo, in_x = lax.rem(z, 4) // 2, 2 * lax.rem(z, 2) + y_hi
    in_place = (y_lo == core) & (y_hi == core) & (in_y_lo == y_lo) & (in_x == x)
    takes_in = (lax.rem(z, 4) // 2 == y_lo) & (lax.rem(z, 2) == x // 2)

    barrier = pltpu.get_barrier_semaphore()

    def greet(device):
        pl.semaphore_signal(barrier, inc=1, device_id=device, device_id_type=MESH)

    greet(partner)
    greet(sibling)
    greet({"y_hi": 1 - y_hi})
    for step in range(1, NZ):
        greet({"z": at_z(step)})
    for step in range(1, 8):
        greet(f_device(at_f(step)))
    for source_x in range(4):
        from_self = (y_hi == core) & (lax.rem(x, 2) == y_hi) & (y_lo == core) & (x == source_x)

        @pl.when(takes_in & jnp.logical_not(from_self))
        def _(source_x=source_x):
            greet({"core": y_hi, "y_hi": lax.rem(x, 2), "y_lo": core, "x": source_x})

    @pl.when(in_place)
    def _():
        pl.semaphore_wait(barrier, 17)

    @pl.when(jnp.logical_not(in_place))
    def _():
        pl.semaphore_wait(barrier, 18)

    my_rows = pl.ds(core * ROWS, ROWS)
    sib_rows = pl.ds((1 - core) * ROWS, ROWS)

    def own_local(j):
        return pltpu.make_async_copy(w_hbm.at[0, j], wbuf.at[z, j, my_rows], r_w.at[j])

    def own_remote(j):
        return remote(
            w_hbm.at[0, j], wbuf.at[z, j, pl.ds(y_hi * ROWS, ROWS)], s_w.at[j], r_w.at[j], partner
        )

    @pl.when(swapped)
    def _():
        for j in range(3):
            own_remote(j).start()

    @pl.when(jnp.logical_not(swapped))
    def _():
        for j in range(3):
            own_local(j).start()

    def ring_copy(direction, k, j, moved):
        sign = 1 - 2 * direction
        slot = at_z(-sign * (k - 1 + moved))
        if k < 4:
            rows = my_rows
        else:
            rows = pl.ds(core * ROWS + direction * (ROWS // 2), ROWS // 2)
        block = wbuf.at[slot, j, rows]
        return remote(
            block, block, s_ring.at[direction, k - 1, j], r_ring.at[direction, k - 1, j], {"z": at_z(sign)}
        )

    def ring(direction, k, j):
        return ring_copy(direction, k, j, 0)

    def landing(direction, k, j):
        return ring_copy(direction, k, j, 1)

    def to_sibling(index, slot, j):
        block = wbuf.at[slot, j, my_rows]
        return remote(block, block, s_sib.at[index, j], r_sib.at[index, j], sibling)

    def from_sibling(index, slot, j):
        block = wbuf.at[slot, j, sib_rows]
        return remote(block, block, s_sib.at[index, j], r_sib.at[index, j], sibling)

    def begin_ring():
        for j in range(3):
            own_local(j).wait()
            ring(0, 1, j).start()
            ring(1, 1, j).start()
            to_sibling(0, z, j).start()

    pl.when(jnp.logical_not(swapped))(begin_ring)

    def wo_in():
        return remote(
            wo_hbm, wo.at[half_in, f], s_wa.at[0], r_wo.at[half_in, f],
            {"core": y_lo, "y_hi": core, "y_lo": in_y_lo, "x": in_x},
        )

    @pl.when(in_place)
    def _():
        pltpu.make_async_copy(wo_hbm, wo.at[half_in, f], r_wo.at[half_in, f]).start()

    @pl.when(jnp.logical_not(in_place))
    def _():
        wo_in().start()

    def level_of(step_index):
        fraction = jnp.full((8, 128), step_index.astype(F32)) / 1000.0
        return (5.0 * fraction / (1.0 + 4.0 * fraction))[0:1, 0:1]

    levels = (level_of(times[0]), level_of(times[core]))
    shift[0:1, :] = cond[pl.ds(pair[0], 1), :]
    shift[1:2, :] = cond[pl.ds(pair[1 - core], 1), :]
    for load in loads:
        load.wait()

    def mixed(p, rows, cols):
        return (1.0 - levels[p]) * lat[rows, cols].astype(F32) + levels[p] * noi[p, rows, cols].astype(F32)

    for p in range(2):

        @pl.loop(0, TOK // 16)
        def _(b, p=p):
            rows = pl.ds(pl.multiple_of(b * 16, 16), 16)
            total = jnp.zeros((16, DZ), F32)
            for q in range(NZ):
                part = mixed(p, rows, pl.ds(q * DZ, DZ))
                total = total + part * part
            mean = jnp.sum(total, axis=1, keepdims=True) * (1.0 / (NZ * DZ))
            inv[p, rows, :] = lax.rsqrt(mean + EPSILON)

    pl.when(swapped)(begin_ring)

    def h_copy(slot):
        return remote(hb.at[0, slot], hb.at[1, slot], s_h.at[slot], r_h.at[slot], partner)

    def distance(i):
        return lax.rem(i + 1, 2) * (-((i + 1) // 2)) + lax.rem(i, 2) * ((i + 1) // 2)

    def make_inputs(first, count):
        @pl.loop(first, first + count)
        def _(i):
            slot = at_z(distance(i))
            cols = pl.ds(pl.multiple_of(slot * DZ, 128), DZ)
            for p in range(2):

                @pl.loop(0, TOK // RB)
                def _(b, p=p):
                    start = pl.multiple_of(b * RB, RB)
                    rows = pl.ds(start, RB)
                    part = mixed(p, rows, cols) * inv[p, rows, :] * gain[:, cols] + shift[p : p + 1, cols]
                    hb[0, slot, pl.ds(p * TOK + start, RB), :] = part.astype(BF16)

            @pl.when(swapped)
            def _():
                h_copy(slot).start()

    acc[...] = jnp.zeros_like(acc)

    def multiply(index, slot):
        for j in range(3):
            from_sibling(index, slot, j).wait_recv()

        @pl.when(swapped)
        def _():
            h_copy(slot).wait_recv()

        @pl.loop(0, 3)
        def _(j):
            acc[j] += jnp.dot(hb[sel, slot], wbuf[slot, j], preferred_element_type=F32)

    groups = [[(0, 0)], [(1, -1), (2, 1)], [(3, -2), (4, 2)], [(5, -3), (6, 3)], [(7, 4)]]
    make_inputs(0, 2)
    for k in range(1, 5):
        for j in range(3):
            for direction in range(2):
                landing(direction, k, j).wait_recv()
                if k < 4:
                    ring(direction, k + 1, j).start()
                    index, step = groups[k][direction]
                    to_sibling(index, at_z(step), j).start()
            if k == 4:
                index, step = groups[k][0]
                to_sibling(index, at_z(step), j).start()
            if k == 1:
                make_inputs(2 + 2 * j, 2)
        for index, step in groups[k - 1]:
            multiply(index, at_z(step))
    for index, step in groups[4]:
        multiply(index, at_z(step))

    my_part = pl.ds(z * TOK, TOK)

    def unit_remote(u):
        return remote(
            units.at[u], ub.at[:, core, my_part], s_a.at[u], r_a.at[z], {"z": owner_of(u)}
        )

    def unit_local(u):
        return pltpu.make_async_copy(units.at[u], ub.at[:, core, my_part], r_a.at[z])

    for u in range(UNITS):
        p, h = u // 3, u % 3
        for j in range(3):
            units[u, j] = acc[j, p * TOK : (p + 1) * TOK, h * HD : (h + 1) * HD].astype(BF16)

        @pl.when(z == owner_of(u))
        def _(u=u):
            unit_local(u).start()

        @pl.when(z != owner_of(u))
        def _(u=u):
            unit_remote(u).start()

    def wo_tick(t, act):
        for half in range(2):
            delta = lax.rem(z - (half * 4 + y_lo * 2 + x // 2) + NZ, NZ)
            b = t - (jnp.minimum(delta, NZ - delta) + 1)

            @pl.when((b >= 0) & (b < 4))
            def _(half=half, delta=delta, b=b):
                slot = core * 4 + b
                block = wo.at[half, slot]

                def copy(lane, device):
                    return remote(block, block, s_wo.at[lane, half, slot], r_wo.at[half, slot], device)

                if act == "send":
                    copy(2, sibling).wait_recv()
                right = (delta <= 2) | ((delta == 3) & (b < 2))
                left = (delta == 0) | (delta >= 6) | ((delta == 5) & (b >= 2))
                for lane, go, device in ((0, right, {"z": at_z(1)}), (1, left, {"z": at_z(-1)})):

                    @pl.when(go)
                    def _(lane=lane, device=device):
                        if act == "send":
                            copy(lane, device).start()
                        else:
                            copy(lane, device).wait_send()

                if act == "send":
                    copy(2, sibling).start()
                else:
                    copy(2, sibling).wait_send()

    is_owner = lax.rem(z, 4) != 3
    mine = jnp.minimum(z - z // 4, UNITS - 1)
    mine_rows = pl.ds(pl.multiple_of((mine // 3) * TOK, TOK), TOK)
    mine_cols = pl.ds(pl.multiple_of(lax.rem(mine, 3) * HD, HD), HD)

    def arrived(source):
        block = ub.at[:, core, pl.ds(source * TOK, TOK)]
        return remote(block, block, s_a.at[0], r_a.at[source], sibling)

    def kv_to_sibling(source, which):
        block = ub.at[pl.ds(1, 2), which, pl.ds(source * TOK, TOK)]
        return remote(block, block, s_kv.at[source], r_kv.at[source], sibling)

    def o_remote(to):
        return remote(ob.at[to], att.at[f, mine_rows, mine_cols], s_o.at[to], r_o.at[mine], {"z": to})

    def o_local(to):
        return pltpu.make_async_copy(ob.at[to], att.at[f, mine_rows, mine_cols], r_o.at[mine])

    @pl.when(is_owner)
    def _():
        @pl.loop(0, NZ)
        def _(i):
            source = at_z(distance(i))
            arrived(source).wait_recv()
            kv_to_sibling(source, core).start()

        @pl.loop(0, NZ)
        def _(i):
            kv_to_sibling(at_z(distance(i)), 1 - core).wait_recv()

    wo_tick(1, "send")

    @pl.loop(0, NZ)
    def _(i):
        to = at_z(distance(NZ - 1 - i))

        @pl.when(is_owner)
        def _():
            queries = ub[0, core, pl.ds(pl.multiple_of(to * TOK, TOK), TOK), :]
            keys = ub[1].reshape(2 * NZ * TOK, HD)
            scores = lax.dot_general(
                queries, keys, (((1,), (1,)), ((), ())), preferred_element_type=F32
            )
            peak = jnp.max(scores, axis=1, keepdims=True)
            weight = jnp.exp2((scores - peak) * (HD**-0.5 * LOG2E))
            mass = jnp.sum(weight, axis=1, keepdims=True)
            result = jnp.dot(
                weight.astype(BF16), ub[2].reshape(2 * NZ * TOK, HD), preferred_element_type=F32
            )
            ob[to] = (result / mass).astype(BF16)

            @pl.when(to == z)
            def _():
                o_local(to).start()

            @pl.when(to != z)
            def _():
                o_remote(to).start()

        @pl.when(lax.rem(i, 3) == 2)
        def _():
            wo_tick(2 + i // 3, "send")

    wo_tick(4, "send")

    def att_copy(source, p, peer):
        block = att.at[source, pl.ds(p * TOK, TOK)]
        return remote(block, block, s_att.at[peer, p], r_att.at[source, p], f_device(peer))

    for p in range(2):
        for h in range(3):
            block = att.at[f, pl.ds(p * TOK, TOK), pl.ds(h * HD, HD)]
            remote(block, block, s_o.at[0], r_o.at[p * 3 + h], sibling).wait_recv()
        for step in (1, 7, 4, 3, 5, 2, 6):
            att_copy(f, p, at_f(step)).start()
        wo_tick(5 + p, "send")
    wo_tick(7, "send")
    wo_tick(8, "send")

    pred[...] = jnp.zeros_like(pred)

    @pl.loop(0, 8)
    def _(step):
        source = at_f(step)

        @pl.when(step > 0)
        def _():
            for p in range(2):
                att_copy(source, p, source).wait_recv()

        for half in range(2):

            @pl.when(source // 4 != core)
            def _(half=half):
                block = wo.at[half, source]
                remote(block, block, s_wo.at[2, half, source], r_wo.at[half, source], sibling).wait_recv()

            pred[half] += lax.dot_general(
                att[source], wo[half, source], (((1,), (1,)), ((), ())), preferred_element_type=F32
            )

    def fin_copy(half):
        return remote(
            pb.at[half], fin.at[y_hi], s_f.at[half], r_f.at[y_hi], {"core": half, "y_hi": core}
        )

    for half in range(2):
        stays = (core == half) & (y_hi == core)
        pb[half] = pred[half].astype(BF16)

        @pl.when(stays)
        def _(half=half):
            pltpu.make_async_copy(pb.at[half], fin.at[y_hi], r_f.at[y_hi]).start()

        @pl.when(jnp.logical_not(stays))
        def _(half=half):
            fin_copy(half).start()

    for section in range(2):
        block = fin.at[section]
        remote(block, block, s_f.at[0], r_f.at[section], sibling).wait_recv()

    @pl.when(swapped)
    def _():
        for j in range(3):
            own_remote(j).wait_send()
        for slot in range(NZ):
            h_copy(slot).wait_send()

    @pl.when(jnp.logical_not(in_place))
    def _():
        wo_in().wait_send()

    for k in range(1, 5):
        for j in range(3):
            for direction in range(2):
                ring(direction, k, j).wait_send()
    for group in groups:
        for index, step in group:
            for j in range(3):
                to_sibling(index, at_z(step), j).wait_send()
    for u in range(UNITS):

        @pl.when(z != owner_of(u))
        def _(u=u):
            unit_remote(u).wait_send()

    @pl.when(is_owner)
    def _():
        for source in range(NZ):
            kv_to_sibling(source, core).wait_send()

            @pl.when(z != source)
            def _(source=source):
                o_remote(source).wait_send()

    @pl.loop(1, 9)
    def _(t):
        wo_tick(t, "wait")

    for p in range(2):
        for step in range(1, 8):
            att_copy(f, p, at_f(step)).wait_send()
    for half in range(2):

        @pl.when(jnp.logical_not((core == half) & (y_hi == core)))
        def _(half=half):
            fin_copy(half).wait_send()


def predictions(times, pair, latents, noise, cond_table, gain, w_qkv, w_out):
    dma = pltpu.SemaphoreType.DMA
    vmem, any_space = pl.BlockSpec(memory_space=pltpu.VMEM), pl.BlockSpec(memory_space=pl.ANY)
    smem = pl.BlockSpec(memory_space=pltpu.SMEM)
    return pl.pallas_call(
        step_kernel,
        out_shape=jax.ShapeDtypeStruct((2, 2 * TOK, ROWS), BF16),
        in_specs=[smem, smem, any_space, any_space, vmem, vmem, any_space, any_space],
        out_specs=vmem,
        scratch_shapes=[
            pltpu.VMEM((TOK, NZ * DZ), BF16),
            pltpu.VMEM((2, TOK, NZ * DZ), BF16),
            pltpu.VMEM((2, NZ * DZ), F32),
            pltpu.VMEM((2, NZ, 2 * TOK, DZ), BF16),
            pltpu.VMEM((2, TOK, 1), F32),
            pltpu.VMEM((NZ, 3, DZ, COLS), BF16),
            pltpu.VMEM((3, 2 * TOK, COLS), F32),
            pltpu.VMEM((UNITS, 3, TOK, HD), BF16),
            pltpu.VMEM((3, 2, NZ * TOK, HD), BF16),
            pltpu.VMEM((NZ, TOK, HD), BF16),
            pltpu.VMEM((8, 2 * TOK, COLS), BF16),
            pltpu.VMEM((2, 8, ROWS, COLS), BF16),
            pltpu.VMEM((2, 2 * TOK, ROWS), F32),
            pltpu.VMEM((2, 2 * TOK, ROWS), BF16),
            dma((3,)),
            dma((3,)), dma((3,)),
            dma((NZ,)), dma((NZ,)),
            dma((2, 4, 3)), dma((2, 4, 3)),
            dma((NZ, 3)), dma((NZ, 3)),
            dma((UNITS,)), dma((NZ,)),
            dma((NZ,)), dma((NZ,)),
            dma((NZ,)), dma((UNITS,)),
            dma((1,)), dma((3, 2, 8)), dma((2, 8)),
            dma((8, 2)), dma((8, 2)),
            dma((2,)), dma((2,)),
        ],
        compiler_params=pltpu.CompilerParams(
            collective_id=0, has_side_effects=True, vmem_limit_bytes=60 * 2**20
        ),
        cost_estimate=pl.CostEstimate(
            flops=9_000_000_000, bytes_accessed=40_000_000, transcendentals=5_000_000
        ),
    )(times, pair, latents, noise, cond_table, gain, w_qkv, w_out)


def body(latents, noise, time_index, cfg_pair, cond_table, gain, w_qkv, w_out):
    found = predictions(
        time_index, cfg_pair, latents, noise, cond_table, gain, w_qkv, jnp.swapaxes(w_out[0], 0, 1)
    )
    sums = found.reshape(2, 2, TOK, ROWS).astype(F32)
    teacher, critic = sums[0], sums[1]
    dmd_grad = critic[0] - (teacher[1] + GUIDANCE * (teacher[0] - teacher[1]))
    col_start = (lax.axis_index("core") * 8 + lax.axis_index("y_lo") * 4 + lax.axis_index("x")) * ROWS
    noise_cols = lax.dynamic_slice_in_dim(noise[1], col_start, ROWS, 1).astype(F32)
    latent_cols = lax.dynamic_slice_in_dim(latents, col_start, ROWS, 1).astype(F32)
    return dmd_grad, critic[1] - (noise_cols - latent_cols)


def solution(mesh):
    torus = Mesh(mesh.devices.reshape(2, NZ, 2, 2, 4), AXES)
    seq, fsdp = ("z", "y_hi"), ("y_lo", "x")
    return jax.shard_map(
        body,
        mesh=torus,
        in_specs=(
            P(seq, None),
            P(None, seq, None),
            P(),
            P(),
            P(),
            P("core", None),
            P("core", None, seq, fsdp),
            P("core", fsdp, seq),
        ),
        out_specs=(P(seq, ("core", *fsdp)), P(seq, ("core", *fsdp))),
        check_vma=False,
    )
```

time: 306 us -> 180 us (0.59)
  waiting for transfers between devices: 78.1 us -> 0 us
  Pallas kernels: 145 us -> 173 us
  local copies, waits for them, and re-layouts: 24.3 us -> 1.54 us
  starting transfers between devices: 17.8 us -> 0 us
  between operations: 18 us -> 0.66 us
  other arithmetic: 14.1 us -> 3.03 us
  matrix products: 6.26 us -> 0 us
    all_to_all x1 -> x0, waiting for transfers between devices: 68.3 us -> none  [body(): blocks = lax.all_to_all(blocks, ('y_lo', 'x'), 0, 0, tiled=True)]
    pallas_call x1, Pallas kernels: 145 us -> 173 us  [predictions(): pl.pallas_call(step_kernel, out_shape=jax.ShapeDtypeStruct((2, 2 * TOK, R...]
    reshape x4 -> x0, local copies, waits for them, and re-layouts: 18.9 us -> none  [the longest x2 17.4 us: body(): blocks = partial_value.reshape(2, TOK, 2, 8, ROWS).transpose(3, 2, 0, 1, 4)]
    ppermute x3 -> x0, starting transfers between devices: 12.6 us -> none  [the longest x1 5.38 us: body(): w_own = lax.ppermute(w_out[0], across, [(0, 0), (1, 2), (2, 1), (3, 3)])]
    ppermute x3 -> x0, waiting for transfers between devices: 9.77 us -> none  [the longest x1 5.7 us: body(): lax.ppermute(sums[y_hi], across, [(0, 0), (1, 2), (2, 1), (3, 3)])]
    reduce_sum x1 -> x0, other arithmetic: 7.48 us -> none  [body(): sums = jnp.sum(blocks.astype(F32), axis=0).astype(BF16)]
    dot_general x1 -> x0, matrix products: 6.26 us -> none  [body(): jnp.einsum('ptc,cd->ptd', attn, out_full, preferred_element_type=F32)]
    all_to_all x1 -> x0, starting transfers between devices: 5.15 us -> none  [body(): blocks = lax.all_to_all(blocks, ('y_lo', 'x'), 0, 0, tiled=True)]
  transfers between devices with their start and end apart: 5 -> 0, of which waited for: 3 -> 0; matrix products, arithmetic and copies ran while one was open for 3% -> 0% of each run, Pallas kernels for 47% -> 0%
where the time goes in v2:
time: 180 us; the launch traced here: 179 us
  Pallas kernels  173 us (96%)
  other arithmetic  3.03 us (2%)
    pallas_call x1, Pallas kernels, predictions(): pl.pallas_call(step_kernel, out_shape=jax.ShapeDtypeStruct((2, 2 * TOK, R...  173 us

profile of v2, /device:TPU:7, one launch (start us, length us, event | category | flops | bytes accessed | tf_op | source)
XLA Modules:
  0.0 178.6 jit_solution(14821002026846254735)
XLA Ops:
  0.6 173.4 %shard_map.95 = bf16[2,384,320]{2,1,0:T(8,128)(2,1)} custom-call(s32[2]{0:T(128)} %times.1, s32[2]{0:T(128)} %pair.1, bf16[192,5120]{1,0:T(8,128)(2,1)} %lat_hbm.1, bf16[2,192,5120]{2,1,0:T(8,128)(2,1)} %noise_hbm.1, f32[16,5120]{1,0:T(8,128)} %cond.1, f32[1,5120]{1,0:T(1,128)} %gain.1, bf16[1,3,320,384]{3,2,1,0:T(8,128)(2,1)} %w_hbm.1, ...), custom_call_target="tpu_custom_call" | custom-call | flops 8999999488 | bytes 40000000 | tf_op jit(solution)/shard_map/pallas_call | solution.py:484
  174.0 1.1 convert.2
  175.2 0.0 slice-start
  175.2 1.5 slice-done
  176.7 1.9 %fusion = (f32[192,320]{1,0:T(8,128)}, f32[192,320]{1,0:T(8,128)}) fusion(f32[2,2,192,320]{3,2,1,0:T(8,128)S(1)} %convert.2, bf16[192,5120]{1,0:T(8,128)(2,1)} %lat_hbm.1, s32[]{:T(128)S(6)} %select_n.4, bf16[1,192,5120]{2,1,0:T(8,128)(2,1)S(1)} %slice-done), kind=kLoop, calls=%fused_computation.1 | loop fusion | flops 491520 | bytes 1720324 | tf_op jit(solution)/shard_map/sub | solution.py:535
Async XLA Ops:
  175.2 1.6 slice-start

commit v3 on v2

--- a/solution.py
+++ b/solution.py
@@ -30,8 +30,8 @@
 
 
 def step_kernel(
-    times, pair, lat_hbm, noise_hbm, cond, gain, w_hbm, wo_hbm, fin,
-    lat, noi, shift, hb, inv, wbuf, acc, units, ub, ob, att, wo, pred, pb,
+    times, pair, lat_hbm, noise_hbm, cond, gain, w_hbm, wo_hbm, dmd, residual,
+    lat, noi, shift, hb, inv, wbuf, acc, units, ub, ob, att, wo, pred, pb, fin, target, base,
     s_in, s_w, r_w, s_h, r_h, s_ring, r_ring, s_sib, r_sib, s_a, r_a, s_kv, r_kv, s_o, r_o,
     s_wa, s_wo, r_wo, s_att, r_att, s_f, r_f,
 ):
@@ -62,6 +62,10 @@
         pltpu.make_async_copy(noise_hbm.at[0], noi.at[0], s_in.at[1]),
         pltpu.make_async_copy(noise_hbm.at[core], noi.at[1], s_in.at[2]),
     ]
+    out_block = core * 8 + f
+    window = pl.ds(pl.multiple_of(((out_block * 5) // 2) * 128, 128), COLS)
+    target_load = pltpu.make_async_copy(noise_hbm.at[1, :, window], target, s_in.at[3])
+    target_load.start()
     for load in loads:
         load.start()
 
@@ -153,19 +157,26 @@
 
     pl.when(jnp.logical_not(swapped))(begin_ring)
 
-    def wo_in():
+    def wo_part(part):
+        return pl.ds(part * (ROWS // 2), ROWS // 2)
+
+    def wo_in(part):
         return remote(
-            wo_hbm, wo.at[half_in, f], s_wa.at[0], r_wo.at[half_in, f],
+            wo_hbm.at[wo_part(part)], wo.at[half_in, f, wo_part(part)], s_wa.at[part], r_wo.at[half_in, f, part],
             {"core": y_lo, "y_hi": core, "y_lo": in_y_lo, "x": in_x},
         )
 
     @pl.when(in_place)
     def _():
-        pltpu.make_async_copy(wo_hbm, wo.at[half_in, f], r_wo.at[half_in, f]).start()
+        for part in range(2):
+            pltpu.make_async_copy(
+                wo_hbm.at[wo_part(part)], wo.at[half_in, f, wo_part(part)], r_wo.at[half_in, f, part]
+            ).start()
 
     @pl.when(jnp.logical_not(in_place))
     def _():
-        wo_in().start()
+        for part in range(2):
+            wo_in(part).start()
 
     def level_of(step_index):
         fraction = jnp.full((8, 128), step_index.astype(F32)) / 1000.0
@@ -280,18 +291,20 @@
             delta = lax.rem(z - (half * 4 + y_lo * 2 + x // 2) + NZ, NZ)
             b = t - (jnp.minimum(delta, NZ - delta) + 1)
 
-            @pl.when((b >= 0) & (b < 4))
+            @pl.when((b >= 0) & (b < 8))
             def _(half=half, delta=delta, b=b):
-                slot = core * 4 + b
-                block = wo.at[half, slot]
+                slot, part = core * 4 + b // 2, lax.rem(b, 2)
+                block = wo.at[half, slot, pl.ds(pl.multiple_of(part * (ROWS // 2), 16), ROWS // 2)]
 
                 def copy(lane, device):
-                    return remote(block, block, s_wo.at[lane, half, slot], r_wo.at[half, slot], device)
+                    return remote(
+                        block, block, s_wo.at[lane, half, b], r_wo.at[half, slot, part], device
+                    )
 
                 if act == "send":
                     copy(2, sibling).wait_recv()
-                right = (delta <= 2) | ((delta == 3) & (b < 2))
-                left = (delta == 0) | (delta >= 6) | ((delta == 5) & (b >= 2))
+                right = (delta <= 2) | ((delta == 3) & (b < 4))
+                left = (delta == 0) | (delta >= 6) | ((delta == 5) & (b >= 4))
                 for lane, go, device in ((0, right, {"z": at_z(1)}), (1, left, {"z": at_z(-1)})):
 
                     @pl.when(go)
@@ -366,25 +379,64 @@
             def _():
                 o_remote(to).start()
 
-        @pl.when(lax.rem(i, 3) == 2)
+        @pl.when(lax.rem(i, 2) == 1)
         def _():
-            wo_tick(2 + i // 3, "send")
-
-    wo_tick(4, "send")
-
-    def att_copy(source, p, peer):
+            wo_tick(2 + i // 2, "send")
+
+    other_f = (1 - y_lo) * 4 + x
+    far_f = y_lo * 4 + lax.rem(x + 2, 4)
+    x_up, x_down, x_far = ({"x": lax.rem(x + step, 4)} for step in (1, 3, 2))
+    y_other = {"y_lo": 1 - y_lo}
+
+    def att_copy(lane, source, p, device):
         block = att.at[source, pl.ds(p * TOK, TOK)]
-        return remote(block, block, s_att.at[peer, p], r_att.at[source, p], f_device(peer))
+        return remote(block, block, s_att.at[lane, p], r_att.at[source, p], device)
+
+    def att_wait(source, p):
+        att_copy(0, source, p, sibling).wait_recv()
+
+    def att_first(p):
+        return [
+            att_copy(lane, f, p, device) for lane, device in enumerate((x_up, x_down, y_other, x_far))
+        ]
+
+    def att_second(p):
+        return [att_copy(4, other_f, p, x_up), att_copy(5, other_f, p, x_down)]
+
+    def att_third(p):
+        return [att_copy(6, far_f, p, y_other)]
 
     for p in range(2):
         for h in range(3):
             block = att.at[f, pl.ds(p * TOK, TOK), pl.ds(h * HD, HD)]
             remote(block, block, s_o.at[0], r_o.at[p * 3 + h], sibling).wait_recv()
-        for step in (1, 7, 4, 3, 5, 2, 6):
-            att_copy(f, p, at_f(step)).start()
-        wo_tick(5 + p, "send")
-    wo_tick(7, "send")
-    wo_tick(8, "send")
+        for copy in att_first(p):
+            copy.start()
+
+    target_load.wait()
+    difference = target[...].astype(F32) - lat[:, window].astype(F32)
+
+    @pl.when(lax.rem(out_block, 2) == 0)
+    def _():
+        base[...] = difference[:, :ROWS]
+
+    @pl.when(lax.rem(out_block, 2) == 1)
+    def _():
+        base[...] = difference[:, COLS - ROWS :]
+
+    wo_tick(6, "send")
+    for p in range(2):
+        att_wait(other_f, p)
+        for copy in att_second(p):
+            copy.start()
+        wo_tick(7 + p, "send")
+    for p in range(2):
+        att_wait(far_f, p)
+        for copy in att_third(p):
+            copy.start()
+        wo_tick(9 + p, "send")
+    wo_tick(11, "send")
+    wo_tick(12, "send")
 
     pred[...] = jnp.zeros_like(pred)
 
@@ -392,17 +444,20 @@
     def _(step):
         source = at_f(step)
 
-        @pl.when(step > 0)
+        @pl.when((source != f) & (source != other_f) & (source != far_f))
         def _():
             for p in range(2):
-                att_copy(source, p, source).wait_recv()
+                att_wait(source, p)
 
         for half in range(2):
 
             @pl.when(source // 4 != core)
             def _(half=half):
-                block = wo.at[half, source]
-                remote(block, block, s_wo.at[2, half, source], r_wo.at[half, source], sibling).wait_recv()
+                for part in range(2):
+                    block = wo.at[half, source, wo_part(part)]
+                    remote(
+                        block, block, s_wo.at[2, half, 0], r_wo.at[half, source, part], sibling
+                    ).wait_recv()
 
             pred[half] += lax.dot_general(
                 att[source], wo[half, source], (((1,), (1,)), ((), ())), preferred_element_type=F32
@@ -429,6 +484,12 @@
         block = fin.at[section]
         remote(block, block, s_f.at[0], r_f.at[section], sibling).wait_recv()
 
+    def found(section, p):
+        return fin[section, p * TOK : (p + 1) * TOK, :].astype(F32)
+
+    dmd[...] = found(1, 0) - (found(0, 1) + GUIDANCE * (found(0, 0) - found(0, 1)))
+    residual[...] = found(1, 1) - base[...]
+
     @pl.when(swapped)
     def _():
         for j in range(3):
@@ -438,7 +499,8 @@
 
     @pl.when(jnp.logical_not(in_place))
     def _():
-        wo_in().wait_send()
+        for part in range(2):
+            wo_in(part).wait_send()
 
     for k in range(1, 5):
         for j in range(3):
@@ -463,13 +525,13 @@
             def _(source=source):
                 o_remote(source).wait_send()
 
-    @pl.loop(1, 9)
+    @pl.loop(1, 13)
     def _(t):
         wo_tick(t, "wait")
 
     for p in range(2):
-        for step in range(1, 8):
-            att_copy(f, p, at_f(step)).wait_send()
+        for copy in att_first(p) + att_second(p) + att_third(p):
+            copy.wait_send()
     for half in range(2):
 
         @pl.when(jnp.logical_not((core == half) & (y_hi == core)))
@@ -477,15 +539,15 @@
             fin_copy(half).wait_send()
 
 
-def predictions(times, pair, latents, noise, cond_table, gain, w_qkv, w_out):
+def outputs(times, pair, latents, noise, cond_table, gain, w_qkv, w_out):
     dma = pltpu.SemaphoreType.DMA
     vmem, any_space = pl.BlockSpec(memory_space=pltpu.VMEM), pl.BlockSpec(memory_space=pl.ANY)
     smem = pl.BlockSpec(memory_space=pltpu.SMEM)
     return pl.pallas_call(
         step_kernel,
-        out_shape=jax.ShapeDtypeStruct((2, 2 * TOK, ROWS), BF16),
+        out_shape=[jax.ShapeDtypeStruct((TOK, ROWS), F32)] * 2,
         in_specs=[smem, smem, any_space, any_space, vmem, vmem, any_space, any_space],
-        out_specs=vmem,
+        out_specs=[vmem, vmem],
         scratch_shapes=[
             pltpu.VMEM((TOK, NZ * DZ), BF16),
             pltpu.VMEM((2, TOK, NZ * DZ), BF16),
@@ -501,7 +563,10 @@
             pltpu.VMEM((2, 8, ROWS, COLS), BF16),
             pltpu.VMEM((2, 2 * TOK, ROWS), F32),
             pltpu.VMEM((2, 2 * TOK, ROWS), BF16),
-            dma((3,)),
+            pltpu.VMEM((2, 2 * TOK, ROWS), BF16),
+            pltpu.VMEM((TOK, COLS), BF16),
+            pltpu.VMEM((TOK, ROWS), F32),
+            dma((4,)),
             dma((3,)), dma((3,)),
             dma((NZ,)), dma((NZ,)),
             dma((2, 4, 3)), dma((2, 4, 3)),
@@ -509,8 +574,8 @@
             dma((UNITS,)), dma((NZ,)),
             dma((NZ,)), dma((NZ,)),
             dma((NZ,)), dma((UNITS,)),
-            dma((1,)), dma((3, 2, 8)), dma((2, 8)),
-            dma((8, 2)), dma((8, 2)),
+            dma((2,)), dma((3, 2, 8)), dma((2, 8, 2)),
+            dma((7, 2)), dma((8, 2)),
             dma((2,)), dma((2,)),
         ],
         compiler_params=pltpu.CompilerParams(
@@ -523,16 +588,11 @@
 
 
 def body(latents, noise, time_index, cfg_pair, cond_table, gain, w_qkv, w_out):
-    found = predictions(
-        time_index, cfg_pair, latents, noise, cond_table, gain, w_qkv, jnp.swapaxes(w_out[0], 0, 1)
+    return tuple(
+        outputs(
+            time_index, cfg_pair, latents, noise, cond_table, gain, w_qkv, jnp.swapaxes(w_out[0], 0, 1)
+        )
     )
-    sums = found.reshape(2, 2, TOK, ROWS).astype(F32)
-    teacher, critic = sums[0], sums[1]
-    dmd_grad = critic[0] - (teacher[1] + GUIDANCE * (teacher[0] - teacher[1]))
-    col_start = (lax.axis_index("core") * 8 + lax.axis_index("y_lo") * 4 + lax.axis_index("x")) * ROWS
-    noise_cols = lax.dynamic_slice_in_dim(noise[1], col_start, ROWS, 1).astype(F32)
-    latent_cols = lax.dynamic_slice_in_dim(latents, col_start, ROWS, 1).astype(F32)
-    return dmd_grad, critic[1] - (noise_cols - latent_cols)
 
 
 def solution(mesh):

time: 180 us -> 179 us (level)
  the two profiles are of different devices: /device:TPU:7 before, /device:TPU:1 now
where the time goes in v3:
time: 179 us
  Pallas kernels  175 us (98%)
  local copies, waits for them, and re-layouts  3.39 us (2%)
    pallas_call x1, Pallas kernels, outputs(): pl.pallas_call(step_kernel, out_shape=[jax.ShapeDtypeStruct((TOK, ROWS),...  175 us

profile of v3, /device:TPU:1, one launch (start us, length us, event | category | flops | bytes accessed | tf_op | source)
XLA Modules:
  0.0 178.6 jit_solution(11744795395497492516)
XLA Ops:
  0.6 174.6 %shard_map.95 = (f32[192,320]{1,0:T(8,128)}, f32[192,320]{1,0:T(8,128)}) custom-call(s32[2]{0:T(128)} %times.1, s32[2]{0:T(128)} %pair.1, bf16[192,5120]{1,0:T(8,128)(2,1)} %lat_hbm.1, bf16[2,192,5120]{2,1,0:T(8,128)(2,1)} %noise_hbm.1, f32[16,5120]{1,0:T(8,128)} %cond.1, f32[1,5120]{1,0:T(1,128)} %gain.1, bf16[1,3,320,384]{3,2,1,0:T(8,128)(2,1)} %w_hbm.1, ...), custom_call_target="tpu_custom_call" | custom-call | flops 8999999488 | bytes 40000000 | tf_op jit(solution)/shard_map/pallas_call | solution.py:546
  175.2 1.7 copy.12
  176.9 1.7 copy.13

commit v4 on v3

--- a/solution.py
+++ b/solution.py
@@ -31,9 +31,9 @@
 
 def step_kernel(
     times, pair, lat_hbm, noise_hbm, cond, gain, w_hbm, wo_hbm, dmd, residual,
-    lat, noi, shift, hb, inv, wbuf, acc, units, ub, ob, att, wo, pred, pb, fin, target, base,
+    lat, noi, shift, hb, inv, wbuf, acc, units, ub, ob, att, wr, wo, pred, pb, fin, target, base,
     s_in, s_w, r_w, s_h, r_h, s_ring, r_ring, s_sib, r_sib, s_a, r_a, s_kv, r_kv, s_o, r_o,
-    s_wa, s_wo, r_wo, s_att, r_att, s_f, r_f,
+    s_wr, r_wr, s_wo, r_wo, s_ws, s_att, r_att, s_f, r_f,
 ):
     core, z, y_hi = lax.axis_index("core"), lax.axis_index("z"), lax.axis_index("y_hi")
     y_lo, x = lax.axis_index("y_lo"), lax.axis_index("x")
@@ -69,11 +69,6 @@
     for load in loads:
         load.start()
 
-    half_in = z // 4
-    in_y_lo, in_x = lax.rem(z, 4) // 2, 2 * lax.rem(z, 2) + y_hi
-    in_place = (y_lo == core) & (y_hi == core) & (in_y_lo == y_lo) & (in_x == x)
-    takes_in = (lax.rem(z, 4) // 2 == y_lo) & (lax.rem(z, 2) == x // 2)
-
     barrier = pltpu.get_barrier_semaphore()
 
     def greet(device):
@@ -86,20 +81,20 @@
         greet({"z": at_z(step)})
     for step in range(1, 8):
         greet(f_device(at_f(step)))
-    for source_x in range(4):
-        from_self = (y_hi == core) & (lax.rem(x, 2) == y_hi) & (y_lo == core) & (x == source_x)
-
-        @pl.when(takes_in & jnp.logical_not(from_self))
-        def _(source_x=source_x):
-            greet({"core": y_hi, "y_hi": lax.rem(x, 2), "y_lo": core, "x": source_x})
-
-    @pl.when(in_place)
-    def _():
-        pl.semaphore_wait(barrier, 17)
-
-    @pl.when(jnp.logical_not(in_place))
-    def _():
-        pl.semaphore_wait(barrier, 18)
+    same = lax.rem(x, 2) == core
+
+    @pl.when(jnp.logical_not(same))
+    def _():
+        for step in range(1, 8):
+            greet({"core": 1 - core, **f_device(at_f(step))})
+
+    @pl.when(same)
+    def _():
+        pl.semaphore_wait(barrier, 20)
+
+    @pl.when(jnp.logical_not(same))
+    def _():
+        pl.semaphore_wait(barrier, 21)
 
     my_rows = pl.ds(core * ROWS, ROWS)
     sib_rows = pl.ds((1 - core) * ROWS, ROWS)
@@ -112,15 +107,23 @@
             w_hbm.at[0, j], wbuf.at[z, j, pl.ds(y_hi * ROWS, ROWS)], s_w.at[j], r_w.at[j], partner
         )
 
+    def wr_own_local():
+        return pltpu.make_async_copy(wo_hbm, wr.at[z], r_wr.at[0, 0])
+
+    def wr_own_remote():
+        return remote(wo_hbm, wr.at[z], s_wr.at[0, 0], r_wr.at[0, 0], partner)
+
     @pl.when(swapped)
     def _():
         for j in range(3):
             own_remote(j).start()
+        wr_own_remote().start()
 
     @pl.when(jnp.logical_not(swapped))
     def _():
         for j in range(3):
             own_local(j).start()
+        wr_own_local().start()
 
     def ring_copy(direction, k, j, moved):
         sign = 1 - 2 * direction
@@ -157,26 +160,56 @@
 
     pl.when(jnp.logical_not(swapped))(begin_ring)
 
-    def wo_part(part):
-        return pl.ds(part * (ROWS // 2), ROWS // 2)
-
-    def wo_in(part):
-        return remote(
-            wo_hbm.at[wo_part(part)], wo.at[half_in, f, wo_part(part)], s_wa.at[part], r_wo.at[half_in, f, part],
-            {"core": y_lo, "y_hi": core, "y_lo": in_y_lo, "x": in_x},
-        )
-
-    @pl.when(in_place)
-    def _():
-        for part in range(2):
-            pltpu.make_async_copy(
-                wo_hbm.at[wo_part(part)], wo.at[half_in, f, wo_part(part)], r_wo.at[half_in, f, part]
-            ).start()
-
-    @pl.when(jnp.logical_not(in_place))
-    def _():
-        for part in range(2):
-            wo_in(part).start()
+    def wr_copy(direction, k, moved):
+        sign = 1 - 2 * direction
+        slot = at_z(-sign * (k - 1 + moved))
+        rows = pl.ds(0, ROWS) if k < 4 else pl.ds(direction * (ROWS // 2), ROWS // 2)
+        block = wr.at[slot, rows]
+        return remote(block, block, s_wr.at[direction, k], r_wr.at[direction, k], {"z": at_z(sign)})
+
+    def wr_out(slot, act):
+        half, to = slot // 4, 2 * lax.rem(slot, 4) + core
+        here = (to == f) & (half == core)
+
+        @pl.when(jnp.logical_not(here))
+        def _():
+            copy = remote(
+                wr.at[slot], wo.at[half, f], s_wo.at[slot], r_wo.at[half, f],
+                {"core": half, **f_device(to)},
+            )
+            if act == "send":
+                copy.start()
+            else:
+                copy.wait_send()
+
+        if act == "send":
+
+            @pl.when(here)
+            def _():
+                pltpu.make_async_copy(wr.at[slot], wo.at[half, f], r_wo.at[half, f]).start()
+
+    def wr_begin():
+        wr_own_local().wait()
+        wr_copy(0, 1, 0).start()
+        wr_copy(1, 1, 0).start()
+        wr_out(z, "send")
+
+    def wr_step(k):
+        for direction in range(2):
+            wr_copy(direction, k, 1).wait_recv()
+            if k < 4:
+                wr_copy(direction, k + 1, 0).start()
+                wr_out(at_z((2 * direction - 1) * k), "send")
+        if k == 4:
+            wr_out(at_z(4), "send")
+
+    def wo_share(source):
+        block = wo.at[core, source]
+        return remote(block, block, s_ws.at[source], r_wo.at[core, source], sibling)
+
+    def wo_forward(source):
+        wo_share(source).wait_recv()
+        wo_share(source).start()
 
     def level_of(step_index):
         fraction = jnp.full((8, 128), step_index.astype(F32)) / 1000.0
@@ -258,6 +291,10 @@
                 to_sibling(index, at_z(step), j).start()
             if k == 1:
                 make_inputs(2 + 2 * j, 2)
+        if k == 3:
+            wr_begin()
+        if k == 4:
+            wr_step(1)
         for index, step in groups[k - 1]:
             multiply(index, at_z(step))
     for index, step in groups[4]:
@@ -286,39 +323,7 @@
         def _(u=u):
             unit_remote(u).start()
 
-    def wo_tick(t, act):
-        for half in range(2):
-            delta = lax.rem(z - (half * 4 + y_lo * 2 + x // 2) + NZ, NZ)
-            b = t - (jnp.minimum(delta, NZ - delta) + 1)
-
-            @pl.when((b >= 0) & (b < 8))
-            def _(half=half, delta=delta, b=b):
-                slot, part = core * 4 + b // 2, lax.rem(b, 2)
-                block = wo.at[half, slot, pl.ds(pl.multiple_of(part * (ROWS // 2), 16), ROWS // 2)]
-
-                def copy(lane, device):
-                    return remote(
-                        block, block, s_wo.at[lane, half, b], r_wo.at[half, slot, part], device
-                    )
-
-                if act == "send":
-                    copy(2, sibling).wait_recv()
-                right = (delta <= 2) | ((delta == 3) & (b < 4))
-                left = (delta == 0) | (delta >= 6) | ((delta == 5) & (b >= 4))
-                for lane, go, device in ((0, right, {"z": at_z(1)}), (1, left, {"z": at_z(-1)})):
-
-                    @pl.when(go)
-                    def _(lane=lane, device=device):
-                        if act == "send":
-                            copy(lane, device).start()
-                        else:
-                            copy(lane, device).wait_send()
-
-                if act == "send":
-                    copy(2, sibling).start()
-                else:
-                    copy(2, sibling).wait_send()
-
+    wr_step(2)
     is_owner = lax.rem(z, 4) != 3
     mine = jnp.minimum(z - z // 4, UNITS - 1)
     mine_rows = pl.ds(pl.multiple_of((mine // 3) * TOK, TOK), TOK)
@@ -350,7 +355,8 @@
         def _(i):
             kv_to_sibling(at_z(distance(i)), 1 - core).wait_recv()
 
-    wo_tick(1, "send")
+
+    wr_step(3)
 
     @pl.loop(0, NZ)
     def _(i):
@@ -379,9 +385,7 @@
             def _():
                 o_remote(to).start()
 
-        @pl.when(lax.rem(i, 2) == 1)
-        def _():
-            wo_tick(2 + i // 2, "send")
+        pl.when(i == 3)(functools.partial(wr_step, 4))
 
     other_f = (1 - y_lo) * 4 + x
     far_f = y_lo * 4 + lax.rem(x + 2, 4)
@@ -424,19 +428,18 @@
     def _():
         base[...] = difference[:, COLS - ROWS :]
 
-    wo_tick(6, "send")
     for p in range(2):
         att_wait(other_f, p)
         for copy in att_second(p):
             copy.start()
-        wo_tick(7 + p, "send")
     for p in range(2):
         att_wait(far_f, p)
         for copy in att_third(p):
             copy.start()
-        wo_tick(9 + p, "send")
-    wo_tick(11, "send")
-    wo_tick(12, "send")
+
+    @pl.loop(0, 8)
+    def _(source):
+        wo_forward(source)
 
     pred[...] = jnp.zeros_like(pred)
 
@@ -449,16 +452,9 @@
             for p in range(2):
                 att_wait(source, p)
 
+        block = wo.at[1 - core, source]
+        remote(block, block, s_ws.at[source], r_wo.at[1 - core, source], sibling).wait_recv()
         for half in range(2):
-
-            @pl.when(source // 4 != core)
-            def _(half=half):
-                for part in range(2):
-                    block = wo.at[half, source, wo_part(part)]
-                    remote(
-                        block, block, s_wo.at[2, half, 0], r_wo.at[half, source, part], sibling
-                    ).wait_recv()
-
             pred[half] += lax.dot_general(
                 att[source], wo[half, source], (((1,), (1,)), ((), ())), preferred_element_type=F32
             )
@@ -494,14 +490,16 @@
     def _():
         for j in range(3):
             own_remote(j).wait_send()
+        wr_own_remote().wait_send()
         for slot in range(NZ):
             h_copy(slot).wait_send()
 
-    @pl.when(jnp.logical_not(in_place))
-    def _():
-        for part in range(2):
-            wo_in(part).wait_send()
-
+    for slot in range(NZ):
+        wr_out(slot, "wait")
+        wo_share(slot).wait_send()
+    for k in range(1, 5):
+        for direction in range(2):
+            wr_copy(direction, k, 0).wait_send()
     for k in range(1, 5):
         for j in range(3):
             for direction in range(2):
@@ -524,10 +522,6 @@
             @pl.when(z != source)
             def _(source=source):
                 o_remote(source).wait_send()
-
-    @pl.loop(1, 13)
-    def _(t):
-        wo_tick(t, "wait")
 
     for p in range(2):
         for copy in att_first(p) + att_second(p) + att_third(p):
@@ -560,6 +554,7 @@
             pltpu.VMEM((3, 2, NZ * TOK, HD), BF16),
             pltpu.VMEM((NZ, TOK, HD), BF16),
             pltpu.VMEM((8, 2 * TOK, COLS), BF16),
+            pltpu.VMEM((NZ, ROWS, COLS), BF16),
             pltpu.VMEM((2, 8, ROWS, COLS), BF16),
             pltpu.VMEM((2, 2 * TOK, ROWS), F32),
             pltpu.VMEM((2, 2 * TOK, ROWS), BF16),
@@ -574,7 +569,7 @@
             dma((UNITS,)), dma((NZ,)),
             dma((NZ,)), dma((NZ,)),
             dma((NZ,)), dma((UNITS,)),
-            dma((2,)), dma((3, 2, 8)), dma((2, 8, 2)),
+            dma((2, 5)), dma((2, 5)), dma((NZ,)), dma((2, 8)), dma((8,)),
             dma((7, 2)), dma((8, 2)),
             dma((2,)), dma((2,)),
         ],

time: 179 us -> 163 us (0.911)
  the two profiles are of different devices: /device:TPU:1 before, /device:TPU:7 now
where the time goes in v4:
time: 163 us; the launch traced here: 162 us
  Pallas kernels  158 us (97%)
  local copies, waits for them, and re-layouts  3.39 us (2%)
    pallas_call x1, Pallas kernels, outputs(): pl.pallas_call(step_kernel, out_shape=[jax.ShapeDtypeStruct((TOK, ROWS),...  158 us
    unnamed x2, local copies, waits for them, and re-layouts  3.39 us

profile of v4, /device:TPU:7, one launch (start us, length us, event | category | flops | bytes accessed | tf_op | source)
XLA Modules:
  0.0 162.4 jit_solution(5163135914723227515)
XLA Ops:
  0.6 158.3 %shard_map.95 = (f32[192,320]{1,0:T(8,128)}, f32[192,320]{1,0:T(8,128)}) custom-call(s32[2]{0:T(128)} %times.1, s32[2]{0:T(128)} %pair.1, bf16[192,5120]{1,0:T(8,128)(2,1)} %lat_hbm.1, bf16[2,192,5120]{2,1,0:T(8,128)(2,1)} %noise_hbm.1, f32[16,5120]{1,0:T(8,128)} %cond.1, f32[1,5120]{1,0:T(1,128)} %gain.1, bf16[1,3,320,384]{3,2,1,0:T(8,128)(2,1)} %w_hbm.1, ...), custom_call_target="tpu_custom_call" | custom-call | flops 8999999488 | bytes 40000000 | tf_op jit(solution)/shard_map/pallas_call | solution.py:540
  159.0 1.7 %copy.12 = f32[192,320]{1,0:T(8,128)} copy(f32[192,320]{1,0:T(8,128)} %get-tuple-element.4) | data formatting | bytes 491520
  160.7 1.7 %copy.13 = f32[192,320]{1,0:T(8,128)} copy(f32[192,320]{1,0:T(8,128)} %get-tuple-element.5) | data formatting | bytes 491520

commit v5 on v4

--- a/solution.py
+++ b/solution.py
@@ -410,78 +410,91 @@
     def att_third(p):
         return [att_copy(6, far_f, p, y_other)]
 
-    for p in range(2):
+    def first(p):
         for h in range(3):
             block = att.at[f, pl.ds(p * TOK, TOK), pl.ds(h * HD, HD)]
             remote(block, block, s_o.at[0], r_o.at[p * 3 + h], sibling).wait_recv()
         for copy in att_first(p):
             copy.start()
 
-    target_load.wait()
-    difference = target[...].astype(F32) - lat[:, window].astype(F32)
-
-    @pl.when(lax.rem(out_block, 2) == 0)
-    def _():
-        base[...] = difference[:, :ROWS]
-
-    @pl.when(lax.rem(out_block, 2) == 1)
-    def _():
-        base[...] = difference[:, COLS - ROWS :]
-
-    for p in range(2):
+    def second(p):
         att_wait(other_f, p)
         for copy in att_second(p):
             copy.start()
-    for p in range(2):
+
+    def third(p):
         att_wait(far_f, p)
         for copy in att_third(p):
             copy.start()
 
+    first(0)
+    first(1)
+    target_load.wait()
+    difference = target[...].astype(F32) - lat[:, window].astype(F32)
+
+    @pl.when(lax.rem(out_block, 2) == 0)
+    def _():
+        base[...] = difference[:, :ROWS]
+
+    @pl.when(lax.rem(out_block, 2) == 1)
+    def _():
+        base[...] = difference[:, COLS - ROWS :]
+
+    second(0)
+    third(0)
+
     @pl.loop(0, 8)
     def _(source):
         wo_forward(source)
 
-    pred[...] = jnp.zeros_like(pred)
-
-    @pl.loop(0, 8)
-    def _(step):
-        source = at_f(step)
-
-        @pl.when((source != f) & (source != other_f) & (source != far_f))
+    second(1)
+    third(1)
+
+    def fin_copy(half, p):
+        return remote(
+            pb.at[half, p], fin.at[y_hi, p], s_f.at[half, p], r_f.at[y_hi, p], {"core": half, "y_hi": core}
+        )
+
+    def send_half(half, p):
+        stays = (core == half) & (y_hi == core)
+
+        @pl.when(stays)
         def _():
-            for p in range(2):
+            pltpu.make_async_copy(pb.at[half, p], fin.at[y_hi, p], r_f.at[y_hi, p]).start()
+
+        @pl.when(jnp.logical_not(stays))
+        def _():
+            fin_copy(half, p).start()
+
+    near = [y_lo * 4 + lax.rem(x + step, 4) for step in (1, 3)]
+    across = [(1 - y_lo) * 4 + lax.rem(x + step, 4) for step in (1, 3, 2)]
+    for p in range(2):
+        rows = pl.ds(p * TOK, TOK)
+        for place, source in enumerate([f, other_f, far_f, *near, *across]):
+            if place > 2:
                 att_wait(source, p)
-
-        block = wo.at[1 - core, source]
-        remote(block, block, s_ws.at[source], r_wo.at[1 - core, source], sibling).wait_recv()
-        for half in range(2):
-            pred[half] += lax.dot_general(
-                att[source], wo[half, source], (((1,), (1,)), ((), ())), preferred_element_type=F32
-            )
-
-    def fin_copy(half):
-        return remote(
-            pb.at[half], fin.at[y_hi], s_f.at[half], r_f.at[y_hi], {"core": half, "y_hi": core}
-        )
-
-    for half in range(2):
-        stays = (core == half) & (y_hi == core)
-        pb[half] = pred[half].astype(BF16)
-
-        @pl.when(stays)
-        def _(half=half):
-            pltpu.make_async_copy(pb.at[half], fin.at[y_hi], r_f.at[y_hi]).start()
-
-        @pl.when(jnp.logical_not(stays))
-        def _(half=half):
-            fin_copy(half).start()
-
-    for section in range(2):
-        block = fin.at[section]
-        remote(block, block, s_f.at[0], r_f.at[section], sibling).wait_recv()
+            if p == 0:
+                block = wo.at[1 - core, source]
+                remote(block, block, s_ws.at[source], r_wo.at[1 - core, source], sibling).wait_recv()
+            for half in range(2):
+                product = lax.dot_general(
+                    att[source, rows], wo[half, source], (((1,), (1,)), ((), ())), preferred_element_type=F32
+                )
+                if place == 0:
+                    pred[half] = product
+                elif place < 7:
+                    pred[half] += product
+                else:
+                    pb[half, p] = (pred[half] + product).astype(BF16)
+                    send_half(half, p)
+
+    for p in range(2):
+        for section in range(2):
+            block = fin.at[section, p]
+            remote(block, block, s_f.at[0, p], r_f.at[section, p], sibling).wait_recv()
 
     def found(section, p):
-        return fin[section, p * TOK : (p + 1) * TOK, :].astype(F32)
+        return fin[section, p].astype(F32)
 
     dmd[...] = found(1, 0) - (found(0, 1) + GUIDANCE * (found(0, 0) - found(0, 1)))
     residual[...] = found(1, 1) - base[...]
@@ -530,7 +543,8 @@
 
         @pl.when(jnp.logical_not((core == half) & (y_hi == core)))
         def _(half=half):
-            fin_copy(half).wait_send()
+            for p in range(2):
+                fin_copy(half, p).wait_send()
 
 
 def outputs(times, pair, latents, noise, cond_table, gain, w_qkv, w_out):
@@ -556,9 +570,9 @@
             pltpu.VMEM((8, 2 * TOK, COLS), BF16),
             pltpu.VMEM((NZ, ROWS, COLS), BF16),
             pltpu.VMEM((2, 8, ROWS, COLS), BF16),
-            pltpu.VMEM((2, 2 * TOK, ROWS), F32),
-            pltpu.VMEM((2, 2 * TOK, ROWS), BF16),
-            pltpu.VMEM((2, 2 * TOK, ROWS), BF16),
+            pltpu.VMEM((2, TOK, ROWS), F32),
+            pltpu.VMEM((2, 2, TOK, ROWS), BF16),
+            pltpu.VMEM((2, 2, TOK, ROWS), BF16),
             pltpu.VMEM((TOK, COLS), BF16),
             pltpu.VMEM((TOK, ROWS), F32),
             dma((4,)),
@@ -571,7 +585,7 @@
             dma((NZ,)), dma((UNITS,)),
             dma((2, 5)), dma((2, 5)), dma((NZ,)), dma((2, 8)), dma((8,)),
             dma((7, 2)), dma((8, 2)),
-            dma((2,)), dma((2,)),
+            dma((2, 2)), dma((2, 2)),
         ],
         compiler_params=pltpu.CompilerParams(
             collective_id=0, has_side_effects=True, vmem_limit_bytes=60 * 2**20

time: 163 us -> 160 us (0.982)
  Pallas kernels: 158 us -> 154 us
    pallas_call x1, Pallas kernels: 158 us -> 154 us  [outputs(): pl.pallas_call(step_kernel, out_shape=[jax.ShapeDtypeStruct((TOK, ROWS),...]
where the time goes in v5:
time: 160 us; the launch traced here: 158 us
  Pallas kernels  154 us (96%)
  local copies, waits for them, and re-layouts  3.39 us (2%)
    pallas_call x1, Pallas kernels, outputs(): pl.pallas_call(step_kernel, out_shape=[jax.ShapeDtypeStruct((TOK, ROWS),...  154 us
    unnamed x2, local copies, waits for them, and re-layouts  3.39 us

profile of v5, /device:TPU:7, one launch (start us, length us, event | category | flops | bytes accessed | tf_op | source)
XLA Modules:
  0.0 157.8 jit_solution(3352295201278901077)
XLA Ops:
  0.6 153.8 %shard_map.95 = (f32[192,320]{1,0:T(8,128)}, f32[192,320]{1,0:T(8,128)}) custom-call(s32[2]{0:T(128)} %times.1, s32[2]{0:T(128)} %pair.1, bf16[192,5120]{1,0:T(8,128)(2,1)} %lat_hbm.1, bf16[2,192,5120]{2,1,0:T(8,128)(2,1)} %noise_hbm.1, f32[16,5120]{1,0:T(8,128)} %cond.1, f32[1,5120]{1,0:T(1,128)} %gain.1, bf16[1,3,320,384]{3,2,1,0:T(8,128)(2,1)} %w_hbm.1, ...), custom_call_target="tpu_custom_call" | custom-call | flops 8999999488 | bytes 40000000 | tf_op jit(solution)/shard_map/pallas_call | solution.py:554
  154.4 1.7 %copy.12 = f32[192,320]{1,0:T(8,128)} copy(f32[192,320]{1,0:T(8,128)} %get-tuple-element.4) | data formatting | bytes 491520
  156.1 1.7 %copy.13 = f32[192,320]{1,0:T(8,128)} copy(f32[192,320]{1,0:T(8,128)} %get-tuple-element.5) | data formatting | bytes 491520

commit v6 on v5

--- a/solution.py
+++ b/solution.py
@@ -33,7 +33,7 @@
     times, pair, lat_hbm, noise_hbm, cond, gain, w_hbm, wo_hbm, dmd, residual,
     lat, noi, shift, hb, inv, wbuf, acc, units, ub, ob, att, wr, wo, pred, pb, fin, target, base,
     s_in, s_w, r_w, s_h, r_h, s_ring, r_ring, s_sib, r_sib, s_a, r_a, s_kv, r_kv, s_o, r_o,
-    s_wr, r_wr, s_wo, r_wo, s_ws, s_att, r_att, s_f, r_f,
+    s_wr, r_wr, s_wo, r_wo, s_ws, s_att, r_att, s_far, r_far, s_f, r_f,
 ):
     core, z, y_hi = lax.axis_index("core"), lax.axis_index("z"), lax.axis_index("y_hi")
     y_lo, x = lax.axis_index("y_lo"), lax.axis_index("x")
@@ -69,6 +69,21 @@
     for load in loads:
         load.start()
 
+    my_rows = pl.ds(core * ROWS, ROWS)
+    sib_rows = pl.ds((1 - core) * ROWS, ROWS)
+
+    def own_local(j):
+        return pltpu.make_async_copy(w_hbm.at[0, j], wbuf.at[z, j, my_rows], r_w.at[j])
+
+    def wr_own_local():
+        return pltpu.make_async_copy(wo_hbm, wr.at[z], r_wr.at[0, 0])
+
+    @pl.when(jnp.logical_not(swapped))
+    def _():
+        for j in range(3):
+            own_local(j).start()
+        wr_own_local().start()
+
     barrier = pltpu.get_barrier_semaphore()
 
     def greet(device):
@@ -96,20 +111,11 @@
     def _():
         pl.semaphore_wait(barrier, 21)
 
-    my_rows = pl.ds(core * ROWS, ROWS)
-    sib_rows = pl.ds((1 - core) * ROWS, ROWS)
-
-    def own_local(j):
-        return pltpu.make_async_copy(w_hbm.at[0, j], wbuf.at[z, j, my_rows], r_w.at[j])
-
     def own_remote(j):
         return remote(
             w_hbm.at[0, j], wbuf.at[z, j, pl.ds(y_hi * ROWS, ROWS)], s_w.at[j], r_w.at[j], partner
         )
 
-    def wr_own_local():
-        return pltpu.make_async_copy(wo_hbm, wr.at[z], r_wr.at[0, 0])
-
     def wr_own_remote():
         return remote(wo_hbm, wr.at[z], s_wr.at[0, 0], r_wr.at[0, 0], partner)
 
@@ -117,13 +123,6 @@
     def _():
         for j in range(3):
             own_remote(j).start()
-        wr_own_remote().start()
-
-    @pl.when(jnp.logical_not(swapped))
-    def _():
-        for j in range(3):
-            own_local(j).start()
-        wr_own_local().start()
 
     def ring_copy(direction, k, j, moved):
         sign = 1 - 2 * direction
@@ -238,6 +237,10 @@
 
     pl.when(swapped)(begin_ring)
 
+    @pl.when(swapped)
+    def _():
+        wr_own_remote().start()
+
     def h_copy(slot):
         return remote(hb.at[0, slot], hb.at[1, slot], s_h.at[slot], r_h.at[slot], partner)
 
@@ -279,6 +282,9 @@
     groups = [[(0, 0)], [(1, -1), (2, 1)], [(3, -2), (4, 2)], [(5, -3), (6, 3)], [(7, 4)]]
     make_inputs(0, 2)
     for k in range(1, 5):
+        if k == 4:
+            for index, step in groups[3]:
+                multiply(index, at_z(step))
         for j in range(3):
             for direction in range(2):
                 landing(direction, k, j).wait_recv()
@@ -295,8 +301,9 @@
             wr_begin()
         if k == 4:
             wr_step(1)
-        for index, step in groups[k - 1]:
-            multiply(index, at_z(step))
+        if k < 4:
+            for index, step in groups[k - 1]:
+                multiply(index, at_z(step))
     for index, step in groups[4]:
         multiply(index, at_z(step))
 
@@ -389,7 +396,8 @@
 
     other_f = (1 - y_lo) * 4 + x
     far_f = y_lo * 4 + lax.rem(x + 2, 4)
-    x_up, x_down, x_far = ({"x": lax.rem(x + step, 4)} for step in (1, 3, 2))
+    x_up, x_down = ({"x": lax.rem(x + step, 4)} for step in (1, 3))
+    left_f, right_f = (y_lo * 4 + lax.rem(x + step, 4) for step in (3, 1))
     y_other = {"y_lo": 1 - y_lo}
 
     def att_copy(lane, source, p, device):
@@ -401,8 +409,17 @@
 
     def att_first(p):
         return [
-            att_copy(lane, f, p, device) for lane, device in enumerate((x_up, x_down, y_other, x_far))
+            att_copy(lane, f, p, device) for lane, device in enumerate((x_up, x_down, y_other))
         ]
+
+    def far_half(lane, source, p):
+        block = att.at[source, pl.ds(p * TOK + lane * (TOK // 2), TOK // 2)]
+        return remote(block, block, s_far.at[lane, p], r_far.at[lane, p], (x_up, x_down)[lane])
+
+    def pass_on(p):
+        for lane, source in ((0, left_f), (1, right_f)):
+            att_wait(source, p)
+            far_half(lane, source, p).start()
 
     def att_second(p):
         return [att_copy(4, other_f, p, x_up), att_copy(5, other_f, p, x_down)]
@@ -423,7 +440,8 @@
             copy.start()
 
     def third(p):
-        att_wait(far_f, p)
+        for lane in range(2):
+            far_half(lane, far_f, p).wait_recv()
         for copy in att_third(p):
             copy.start()
 
@@ -440,6 +458,7 @@
     def _():
         base[...] = difference[:, COLS - ROWS :]
 
+    pass_on(0)
     second(0)
     third(0)
 
@@ -447,6 +466,7 @@
     def _(source):
         wo_forward(source)
 
+    pass_on(1)
     second(1)
     third(1)
 
@@ -471,7 +491,7 @@
     for p in range(2):
         rows = pl.ds(p * TOK, TOK)
         for place, source in enumerate([f, other_f, far_f, *near, *across]):
-            if place > 2:
+            if place > 4:
                 att_wait(source, p)
             if p == 0:
                 block = wo.at[1 - core, source]
@@ -537,6 +557,8 @@
                 o_remote(source).wait_send()
 
     for p in range(2):
+        far_half(0, left_f, p).wait_send()
+        far_half(1, right_f, p).wait_send()
         for copy in att_first(p) + att_second(p) + att_third(p):
             copy.wait_send()
     for half in range(2):
@@ -586,6 +608,7 @@
             dma((2, 5)), dma((2, 5)), dma((NZ,)), dma((2, 8)), dma((8,)),
             dma((7, 2)), dma((8, 2)),
             dma((2, 2)), dma((2, 2)),
+            dma((2, 2)), dma((2, 2)),
         ],
         compiler_params=pltpu.CompilerParams(
             collective_id=0, has_side_effects=True, vmem_limit_bytes=60 * 2**20

time: 160 us -> 159 us (level); the launches traced: 158 us -> 159 us
  no operation moved by 1% of the time
where the time goes in v6:
time: 159 us
  Pallas kernels  155 us (97%)
  local copies, waits for them, and re-layouts  3.39 us (2%)
    pallas_call x1, Pallas kernels, outputs(): pl.pallas_call(step_kernel, out_shape=[jax.ShapeDtypeStruct((TOK, ROWS),...  155 us
    unnamed x2, local copies, waits for them, and re-layouts  3.39 us

profile of v6, /device:TPU:7, one launch (start us, length us, event | category | flops | bytes accessed | tf_op | source)
XLA Modules:
  0.0 159.0 jit_solution(1367917406190538725)
XLA Ops:
  0.6 155.0 %shard_map.95 = (f32[192,320]{1,0:T(8,128)}, f32[192,320]{1,0:T(8,128)}) custom-call(s32[2]{0:T(128)} %times.1, s32[2]{0:T(128)} %pair.1, bf16[192,5120]{1,0:T(8,128)(2,1)} %lat_hbm.1, bf16[2,192,5120]{2,1,0:T(8,128)(2,1)} %noise_hbm.1, f32[16,5120]{1,0:T(8,128)} %cond.1, f32[1,5120]{1,0:T(1,128)} %gain.1, bf16[1,3,320,384]{3,2,1,0:T(8,128)(2,1)} %w_hbm.1, ...), custom_call_target="tpu_custom_call" | custom-call | flops 8999999488 | bytes 40000000 | tf_op jit(solution)/shard_map/pallas_call | solution.py:576
  155.6 1.7 %copy.12 = f32[192,320]{1,0:T(8,128)} copy(f32[192,320]{1,0:T(8,128)} %get-tuple-element.4) | data formatting | bytes 491520
  157.3 1.7 %copy.13 = f32[192,320]{1,0:T(8,128)} copy(f32[192,320]{1,0:T(8,128)} %get-tuple-element.5) | data formatting | bytes 491520

commit v7 on v6

--- a/solution.py
+++ b/solution.py
@@ -409,7 +409,7 @@
 
     def att_first(p):
         return [
-            att_copy(lane, f, p, device) for lane, device in enumerate((x_up, x_down, y_other))
+            att_copy(lane, f, p, device) for lane, device in enumerate((y_other, x_up, x_down))
         ]
 
     def far_half(lane, source, p):

time: 159 us -> 159 us (level)
  no operation moved by 1% of the time
where the time goes in v7:
time: 159 us
  Pallas kernels  155 us (97%)
  local copies, waits for them, and re-layouts  3.39 us (2%)
    pallas_call x1, Pallas kernels, outputs(): pl.pallas_call(step_kernel, out_shape=[jax.ShapeDtypeStruct((TOK, ROWS),...  155 us
    unnamed x2, local copies, waits for them, and re-layouts  3.39 us

profile of v7, /device:TPU:7, one launch (start us, length us, event | category | flops | bytes accessed | tf_op | source)
XLA Modules:
  0.0 159.0 jit_solution(6273302339567108462)
XLA Ops:
  0.6 155.0 %shard_map.95 = (f32[192,320]{1,0:T(8,128)}, f32[192,320]{1,0:T(8,128)}) custom-call(s32[2]{0:T(128)} %times.1, s32[2]{0:T(128)} %pair.1, bf16[192,5120]{1,0:T(8,128)(2,1)} %lat_hbm.1, bf16[2,192,5120]{2,1,0:T(8,128)(2,1)} %noise_hbm.1, f32[16,5120]{1,0:T(8,128)} %cond.1, f32[1,5120]{1,0:T(1,128)} %gain.1, bf16[1,3,320,384]{3,2,1,0:T(8,128)(2,1)} %w_hbm.1, ...), custom_call_target="tpu_custom_call" | custom-call | flops 8999999488 | bytes 40000000 | tf_op jit(solution)/shard_map/pallas_call | solution.py:576
  155.6 1.7 %copy.12 = f32[192,320]{1,0:T(8,128)} copy(f32[192,320]{1,0:T(8,128)} %get-tuple-element.4) | data formatting | bytes 491520
  157.3 1.7 %copy.13 = f32[192,320]{1,0:T(8,128)} copy(f32[192,320]{1,0:T(8,128)} %get-tuple-element.5) | data formatting | bytes 491520
